TPU v7x, 512 devices: a whole 4x4x16 slice. The times are simulated.
512 devices in a mesh: row: 16 (over y, x), blk: 32 (over z, core).
Axes of the slice: x: 4, y: 4, z: 16, core: 2. Of those that a mesh axis runs over, the one named last changes fastest.
Arguments:
- gradient: bfloat16 [4096, 4096], P('row', 'blk'), may hold values from -1.5 to 1.5
- slot_jobs: int32 [32, 2], P('blk'), may hold values from 0 to 40, as said below
- old_stats: float32 [32, 1024, 1024], P('blk', 'row'), may hold values from -1.2 to 1.2
Outputs:
- new_stats: float32 [32, 1024, 1024], P('blk', 'row')
Inputs may be any that keep to these rules, and one draw needn't show every extreme that they name: `slot_jobs`: each code below 40 appears in exactly one slot; 40 marks an empty slot.
All inputs are finite; a program needn't handle non-finite values.
Results may differ from a plain program's by a relative error of at most 0.0003.
Values may be sent and summed in bfloat16 or wider, within the bound.
No kernel may reach another device: no remote copies, remote signals or barrier semaphores. Data moves between devices by JAX's collectives and lax.ppermute only.
A program may use at most 64 MiB of HBM per device.

v0:
```python
import jax
import jax.numpy as jnp
import numpy as np
from jax import lax
from jax.sharding import PartitionSpec as P

TILE = 1024
NT = 4
HALF = 512
UT = 10


def slot_term(job_code, rows_all, column_set):
    per_kind = 2 * UT
    upper_i, upper_j = np.triu_indices(NT)
    table_i = jnp.asarray(upper_i.astype(np.int32))
    table_j = jnp.asarray(upper_j.astype(np.int32))
    gram_kind = jnp.minimum(job_code // per_kind, 2)
    within = job_code % per_kind
    tile_id = within // 2
    half_index = within % 2
    start_row = table_i[tile_id] * TILE + half_index * HALF
    start_col = table_j[tile_id] * TILE

    def left_gram():
        panel_row = lax.dynamic_slice_in_dim(column_set, start_row, HALF, 0)
        panel_col = lax.dynamic_slice_in_dim(column_set, start_col, TILE, 0)
        return lax.dot_general(
            panel_row, panel_col, (((1,), (1,)), ((), ())), preferred_element_type=jnp.float32
        )

    def right_gram():
        panel_row = lax.dynamic_slice_in_dim(rows_all, start_row, HALF, 1)
        panel_col = lax.dynamic_slice_in_dim(rows_all, start_col, TILE, 1)
        return lax.dot_general(
            panel_row, panel_col, (((0,), (0,)), ((), ())), preferred_element_type=jnp.float32
        )

    def empty_slot():
        return jnp.zeros((HALF, TILE), jnp.float32)

    return lax.switch(gram_kind, [left_gram, right_gram, empty_slot])


def per_device(gradient, slot_jobs, old_stats):
    rows_all = lax.all_gather(gradient, "blk", axis=1, tiled=True)
    narrow = lax.all_to_all(gradient, "row", split_axis=1, concat_axis=0, tiled=True)
    column_set = lax.all_gather(narrow, "blk", axis=1, tiled=True)
    slot_count = slot_jobs.shape[1]
    terms = jnp.concatenate(
        [slot_term(slot_jobs[0, slot], rows_all, column_set) for slot in range(slot_count)], axis=0
    )
    summed = lax.psum_scatter(
        lax.slice_in_dim(terms, 0, old_stats.shape[1] * lax.axis_size("row"), axis=0),
        "row",
        scatter_dimension=0,
        tiled=True,
    )
    return 0.95 * old_stats + 0.05 * summed[None]


def solution(mesh):
    placed = (P("row", "blk"), P("blk", None), P("blk", "row", None))
    return jax.shard_map(
        per_device, mesh=mesh, in_specs=placed, out_specs=P("blk", "row", None), check_vma=False
    )
```

profile of v0, /device:TPU:1, one launch (start us, length us, event | category | flops | bytes accessed | tf_op | source)
XLA Modules:
  0.0 269.5 jit_solution(4555276508204091385)
XLA Ops:
  6.5 0.0 all-gather.5.cloned.1.call-start
  6.5 0.7 all-gather.5.cloned.1.call-update
  7.3 0.0 all-gather.3.cloned.1.call-start
  7.3 0.9 copy.10
  8.2 14.0 %all_to_all.19 = bf16[256,16,8]{0,2,1:T(8,128)(2,1)} all-to-all(bf16[256,16,8]{0,2,1:T(8,128)(2,1)S(1)} %bitcast.17), channel_id=1, replica_groups=mesh['row'=16,'blk'=32] {'row'}, dimensions={1} | all-to-all | bytes 131072 | tf_op jit(solution)/shard_map/all_to_all | solution.py:47
  22.3 0.0 all-gather.3.cloned.1.call-update
  22.3 0.0 reduce-scatter.2.cloned.1.call-start
  22.3 1.4 fusion.18
  27.7 1.4 fusion.16
  31.7 57.1 %all-gather.5.cloned.1.call-done = bf16[256,4096]{1,0:T(8,128)(2,1)} async-done(((bf16[256,128]{1,0:T(8,128)(2,1)}), bf16[256,4096]{1,0:T(8,128)(2,1)}) %all-gather.5.cloned.1.call-update) | async-done | bytes 2097168 | tf_op jit(solution)/shard_map/all_gather | solution.py:46
  88.8 69.8 %all-gather.3.cloned.1.call-done = bf16[4096,256]{0,1:T(8,128)(2,1)} async-done(((bf16[4096,8]{0,1:T(8,128)(2,1)}), bf16[4096,256]{0,1:T(8,128)(2,1)}) %all-gather.3.cloned.1.call-update) | async-done | bytes 2097168 | tf_op jit(solution)/shard_map/all_gather | solution.py:48
  158.5 0.2 conditional.2
  158.5 0.2 broadcast.9
  158.8 7.1 %conditional.3 = (f32[512,1024]{1,0:T(8,128)}) conditional(s32[]{:T(128)} %clamp.7, (s32[]{:T(128)}, bf16[4096,256]{0,1:T(8,128)(2,1)}, s32[]{:T(128)}) %tuple.26, (s32[]{:T(128)}, bf16[256,4096]{1,0:T(8,128)(2,1)}, s32[]{:T(128)}) %tuple.27, () %tuple.28), branch_computations={%region_3.4_spmd, %region_4.5_spmd, %region_5.6_spmd} | conditional | flops 268435456 | bytes 7077972 | solution.py:42
  158.8 4.1 %copy.12 = bf16[4096,256]{1,0:T(8,128)(2,1)} copy(bf16[4096,256]{0,1:T(8,128)(2,1)} %get-tuple-element.53) | data formatting | bytes 4194304 | tf_op jit(solution)/shard_map
  162.9 3.0 %fusion.8 = f32[512,1024]{1,0:T(8,128)} fusion(bf16[4096,256]{1,0:T(8,128)(2,1)} %copy.12, s32[]{:T(128)S(6)} %select_n.51, s32[]{:T(128)S(6)} %select_n.50), kind=kOutput, calls=%fused_computation.8 | convolution fusion | flops 268435456 | bytes 2883592 | tf_op jit(solution)/shard_map/cond/branch_0_fun/dot_general | solution.py:28
  165.8 4.1 %pad_maximum_fusion = f32[1024,1024]{1,0:T(8,128)} fusion(f32[512,1024]{1,0:T(8,128)} %get-tuple-element.64, f32[512,1024]{1,0:T(8,128)S(1)} %get-tuple-element.63), kind=kLoop, calls=%fused_computation.16 | loop fusion | flops 1048576 | bytes 8388608 | tf_op jit(solution)/shard_map/concatenate | solution.py:50
  169.9 0.0 copy-start
  169.9 0.0 reduce-scatter.2.cloned.1.call-update
  170.0 91.3 %reduce-scatter.2.cloned.1.call-done = f32[64,1024]{1,0:T(8,128)} async-done(((f32[1024,1024]{1,0:T(8,128)}), f32[64,1024]{1,0:T(8,128)}) %reduce-scatter.2.cloned.1.call-update) | async-done | bytes 262160 | tf_op jit(solution)/shard_map/reduce_scatter | solution.py:53
  261.3 0.0 copy-done
  261.3 1.7 bitcast_add_fusion
Async XLA Ops:
  6.5 82.2 %all-gather.5.cloned.1.call-start = ((), (), s32[]{:S(2)}) async-start(), calls=%async_computation.3 | async-start | bytes 2162688 | tf_op jit(solution)/shard_map/all_gather | solution.py:46
  7.3 151.3 %all-gather.3.cloned.1.call-start = ((), (), s32[]{:S(2)}) async-start(), calls=%async_computation.2 | async-start | bytes 2162688 | tf_op jit(solution)/shard_map/all_gather | solution.py:48
  22.3 239.0 %reduce-scatter.2.cloned.1.call-start = ((), (), s32[]{:S(2)}) async-start(), calls=%async_computation.4 | async-start | bytes 4456448 | tf_op jit(solution)/shard_map/reduce_scatter | solution.py:53
  169.9 91.3 %copy-start = (f32[1,64,1024]{2,1,0:T(8,128)S(1)}, f32[1,64,1024]{2,1,0:T(8,128)}, u32[]{:S(2)}) copy-start(f32[1,64,1024]{2,1,0:T(8,128)} %param.15) | copy-start | bytes 786436
Sparse Core Ops, SparseCore 0:
  9.4 79.3 all-gather.4
  90.9 67.5 all-gather.2
  170.1 91.1 reduce-scatter.1
where the time goes:
time: 271 us; the launch traced here: 269 us
  waiting for transfers between devices  219 us (81%)
  between operations  19.7 us (7%)
  blocking collectives  14 us (5%)
  local copies, waits for them, and re-layouts  8.06 us (3%)
  other arithmetic  5.79 us (2%)
  matrix products  2.95 us (1%)
    reduce_scatter x1, waiting for transfers between devices, per_device(): lax.psum_scatter(lax.slice_in_dim(terms, 0, old_stats.shape[1] * lax.axis...  91.3 us
    all_gather x1, waiting for transfers between devices, per_device(): column_set = lax.all_gather(narrow, 'blk', axis=1, tiled=True)  69.8 us
    all_gather x1, waiting for transfers between devices, per_device(): rows_all = lax.all_gather(gradient, 'blk', axis=1, tiled=True)  57.1 us
    all_to_all x1, blocking collectives, per_device(): lax.all_to_all(gradient, 'row', split_axis=1, concat_axis=0, tiled=True)  14 us
  transfers between devices with their start and end apart: 3, of which 3 were waited for; matrix products, arithmetic and copies ran while one was open for 1% of the time, Pallas kernels for 0%

commit v1 on v0

v1 whole, which is shorter than its diff:
```python
import jax
import jax.numpy as jnp
import numpy as np
from jax import lax
from jax.sharding import PartitionSpec as P

TILE = 1024
NT = 4
HALF = 512
UT = 10
LANES = 128
GAIN = 2.0**15


def panels(gradient):
    rows, cols = gradient.shape
    n_row = lax.axis_size("row")
    n_blk = lax.axis_size("blk")
    depth = cols // n_row
    scaled = gradient.astype(jnp.float32) * GAIN
    largest = jnp.max(jnp.abs(scaled))
    scaled = scaled.astype(jnp.float16)
    out = scaled.T.reshape(n_row, depth, rows)
    mark = jnp.broadcast_to(largest.astype(jnp.float16), out.shape)
    got = lax.all_to_all(jnp.concatenate([out, mark], axis=1), "row", split_axis=0, concat_axis=0, tiled=True)
    narrow = got[:, :depth].reshape(n_row, depth, rows // LANES, LANES)
    narrow = narrow.transpose(0, 2, 1, 3).reshape(rows, cols)
    largest = jnp.max(got[:, depth:])
    mark = jnp.broadcast_to(largest, (16, cols))
    every = lax.all_gather(jnp.concatenate([scaled, narrow, mark], axis=0), "blk", axis=0, tiled=False)
    largest = jnp.max(every[:, 2 * rows :].astype(jnp.float32))
    right = every[:, :rows].astype(jnp.bfloat16)
    left = every[:, rows : 2 * rows].astype(jnp.bfloat16).reshape(n_blk, n_blk, depth, LANES)
    left = left.transpose(1, 0, 2, 3).reshape(n_blk, rows, LANES)
    return jnp.stack([left, right]), largest


def slot_term(job_code, both):
    per_kind = 2 * UT
    upper_i, upper_j = np.triu_indices(NT)
    table_i = jnp.asarray(upper_i.astype(np.int32))
    table_j = jnp.asarray(upper_j.astype(np.int32))
    gram_kind = jnp.minimum(job_code // per_kind, 1)
    within = job_code % per_kind
    tile_id = within // 2
    half_index = within % 2
    start_row = (table_i[tile_id] * TILE + half_index * HALF) // LANES
    start_col = (table_j[tile_id] * TILE) // LANES
    zero = jnp.zeros_like(gram_kind)
    depth = both.shape[2]
    panel_row = lax.dynamic_slice(both, (gram_kind, start_row, zero, zero), (1, HALF // LANES, depth, LANES))[0]
    panel_col = lax.dynamic_slice(both, (gram_kind, start_col, zero, zero), (1, TILE // LANES, depth, LANES))[0]
    panel_row = panel_row.transpose(1, 0, 2).reshape(depth, HALF)
    panel_col = panel_col.transpose(1, 0, 2).reshape(depth, TILE)
    return lax.dot_general(panel_row, panel_col, (((0,), (0,)), ((), ())), preferred_element_type=jnp.float32)


def per_device(gradient, slot_jobs, old_stats):
    both, largest = panels(gradient)
    slot_count = slot_jobs.shape[1]
    share = old_stats.shape[1]
    n_row = lax.axis_size("row")
    largest = jnp.maximum(largest, 2.0**-24)
    unit = largest * largest * (both.shape[2] / 2.0**15)
    terms = [(slot_term(slot_jobs[0, slot], both) / unit).astype(jnp.float16) for slot in range(slot_count)]
    terms = jnp.concatenate(terms, axis=0).reshape(n_row, share, TILE)
    got = lax.all_to_all(terms, "row", split_axis=0, concat_axis=0, tiled=True)
    summed = jnp.sum(got.astype(jnp.float32), axis=0)
    slot = lax.axis_index("row") // (n_row // slot_count)
    used = slot_jobs[0, slot] < 4 * UT
    summed = jnp.where(used, summed * (unit * GAIN**-2), 0.0)
    return 0.95 * old_stats + 0.05 * summed[None]


def solution(mesh):
    placed = (P("row", "blk"), P("blk", None), P("blk", "row", None))
    return jax.shard_map(
        per_device, mesh=mesh, in_specs=placed, out_specs=P("blk", "row", None), check_vma=False
    )
```

time: 271 us -> 127 us (0.47)
  waiting for transfers between devices: 219 us -> 32.3 us
  blocking collectives: 14 us -> 51.3 us
  starting transfers between devices: 0.08 us -> 14.5 us
  between operations: 19.7 us -> 8.49 us
  other arithmetic: 5.79 us -> 9.83 us
    all_gather x2 -> x0, waiting for transfers between devices: 127 us -> none  [the longest x1 69.8 us: per_device(): column_set = lax.all_gather(narrow, 'blk', axis=1, tiled=True)]
    reduce_scatter x1 -> x0, waiting for transfers between devices: 91.3 us -> none  [per_device(): lax.psum_scatter(lax.slice_in_dim(terms, 0, old_stats.shape[1] * lax.axis...]
    all_gather x0 -> x1, blocking collectives: none -> 51.3 us  [panels(): lax.all_gather(jnp.concatenate([scaled, narrow, mark], axis=0), 'blk', ax...]
    all_to_all x0 -> x2, waiting for transfers between devices: none -> 32.3 us  [the longest x1 32.3 us: per_device(): got = lax.all_to_all(terms, 'row', split_axis=0, concat_axis=0, tiled=True)]
    all_to_all x0 -> x2, starting transfers between devices: none -> 14.5 us  [the longest x1 7.58 us: panels(): lax.all_to_all(jnp.concatenate([out, mark], axis=1), 'row', split_axis=0,...]
    all_to_all x1 -> x0, blocking collectives: 14 us -> none  [per_device(): lax.all_to_all(gradient, 'row', split_axis=1, concat_axis=0, tiled=True)]
    transpose x0 -> x3, other arithmetic: none -> 4.68 us  [the longest x1 3.13 us: panels(): left = left.transpose(1, 0, 2, 3).reshape(n_blk, rows, LANES)]
    another operation x2 -> x0, local copies, waits for them, and re-layouts: 4.32 us -> none
  transfers between devices with their start and end apart: 3 -> 2, of which waited for: 3 -> 1; matrix products, arithmetic and copies ran while one was open for 1% -> 2% of each run, Pallas kernels for 0% -> 0%
where the time goes in v1:
time: 127 us
  blocking collectives  51.3 us (40%)
  waiting for transfers between devices  32.3 us (25%)
  starting transfers between devices  14.5 us (11%)
  other arithmetic  9.83 us (8%)
  local copies, waits for them, and re-layouts  9.73 us (8%)
  between operations  8.49 us (7%)
    all_gather x1, blocking collectives, panels(): lax.all_gather(jnp.concatenate([scaled, narrow, mark], axis=0), 'blk', ax...  51.3 us
    all_to_all x1, waiting for transfers between devices, per_device(): got = lax.all_to_all(terms, 'row', split_axis=0, concat_axis=0, tiled=True)  32.3 us
    all_to_all x1, starting transfers between devices, panels(): lax.all_to_all(jnp.concatenate([out, mark], axis=1), 'row', split_axis=0,...  7.58 us
    all_to_all x1, starting transfers between devices, per_device(): got = lax.all_to_all(terms, 'row', split_axis=0, concat_axis=0, tiled=True)  6.88 us
    transpose x1, other arithmetic, panels(): left = left.transpose(1, 0, 2, 3).reshape(n_blk, rows, LANES)  3.13 us
  transfers between devices with their start and end apart: 2, of which 1 were waited for; matrix products, arithmetic and copies ran while one was open for 2% of the time, Pallas kernels for 0%

profile of v1, /device:TPU:1, one launch (start us, length us, event | category | flops | bytes accessed | tf_op | source)
XLA Modules:
  0.0 127.0 jit_solution(9232734440623899062)
XLA Ops:
  0.0 0.9 copy.28
  0.9 0.6 fusion.10
  2.2 0.7 concatenate.9
  2.9 7.6 %all-to-all-start = ((f16[16,16,256]{2,1,0:T(8,128)(2,1)}), f16[16,16,256]{2,1,0:T(8,128)(2,1)S(1)}, u32[]{:S(2)}, u32[]{:S(2)}) async-start(f16[16,16,256]{2,1,0:T(8,128)(2,1)} %concatenate.9), calls=%async_computation | async-start | bytes 262144 | tf_op jit(solution)/shard_map/all_to_all | solution.py:25
  10.5 1.4 %constant_dynamic-slice_fusion = (s32[1,1]{1,0:T(1,128)}, s32[1,1]{1,0:T(1,128)}, s32[1,1]{1,0:T(1,128)}) fusion(s32[1,2]{1,0:T(1,128)} %param.8, s32[]{:T(128)S(6)} %select_n.95), kind=kLoop, calls=%fused_computation.32 | loop fusion | bytes 28 | tf_op jit(solution)/shard_map/dynamic_slice | solution.py:70
  15.8 1.4 %fusion.12 = (s32[1]{0:T(128)}, s32[1]{0:T(128)}, s32[1]{0:T(128)}, s32[1]{0:T(128)}) fusion(s32[10]{0:T(128)} %constant.148.clone, s32[]{:T(128)S(6)} %select_n.101, s32[]{:T(128)S(6)} %select_n.111, s32[10]{0:T(128)} %constant.147.clone), kind=kLoop, calls=%fused_computation.34 | loop fusion | bytes 40 | tf_op jit(solution)/shard_map/dynamic_slice | solution.py:48
  19.7 0.0 all-to-all-done
  19.7 0.6 slice_reduce_fusion
  20.4 0.1 copy.29
  20.5 0.7 broadcast_in_dim.9
  21.2 0.1 maximum_maximum_fusion
  21.2 0.2 copy.30
  21.4 51.3 %all-gather.2 = f16[16896,128]{1,0:T(8,128)(2,1)S(1)} all-gather(f16[528,128]{1,0:T(8,128)(2,1)S(1)} %copy.30), channel_id=2, replica_groups=mesh['row'=16,'blk'=32] {'blk'}, dimensions={0}, use_global_device_ids=true | all-gather | bytes 4460544 | tf_op jit(solution)/shard_map/all_gather | solution.py:30
  72.7 0.7 convert_reduce_fusion.1
  73.3 3.1 %fusion.1 = (bf16[32,32,8,128]{3,2,0,1:T(8,128)(2,1)}, bf16[1,32,256,128]{3,2,1,0:T(8,128)(2,1)}) fusion(f16[32,528,128]{2,1,0:T(8,128)(2,1)S(1)} %bitcast.60), kind=kLoop, calls=%fused_computation.12 | loop fusion | flops 2097152 | bytes 8388608 | tf_op jit(solution)/shard_map/transpose | solution.py:34
  77.1 0.0 copy-start
  77.1 2.3 %copy.37 = bf16[32,32,8,128]{3,2,1,0:T(8,128)(2,1)S(1)} copy(bf16[32,32,8,128]{3,2,0,1:T(8,128)(2,1)} %get-tuple-element.5) | data formatting | bytes 4194304 | tf_op jit(solution)/shard_map/transpose | solution.py:34
  79.5 0.0 copy-done
  79.5 0.4 fusion.4
  79.9 1.0 copy.33
  80.9 1.1 fusion.9
  82.0 0.0 copy-start.1
  82.0 0.1 copy.32
  82.2 0.1 copy.34
  82.3 0.2 copy.35
  82.6 0.5 copy-done.1
  83.1 0.5 divide_convert_fusion.1
  83.5 0.5 divide_convert_fusion
  84.0 2.0 %pad_maximum_fusion = f16[1024,1024]{1,0:T(8,128)(2,1)} fusion(f16[512,1024]{1,0:T(8,128)(2,1)S(1)} %divide_convert_fusion, f16[512,1024]{1,0:T(8,128)(2,1)S(1)} %divide_convert_fusion.1), kind=kLoop, calls=%fused_computation.13 | loop fusion | flops 1048576 | bytes 4194304 | tf_op jit(solution)/shard_map/concatenate | solution.py:66
  86.0 6.9 %all-to-all-start.1 = ((f16[16,64,1024]{2,1,0:T(8,128)(2,1)}), f16[16,64,1024]{2,1,0:T(8,128)(2,1)S(1)}, u32[]{:S(2)}, u32[]{:S(2)}) async-start(f16[16,64,1024]{2,1,0:T(8,128)(2,1)} %bitcast.61), calls=%async_computation.1 | async-start | bytes 4194304 | tf_op jit(solution)/shard_map/all_to_all | solution.py:67
  92.9 0.0 copy-start.2
  93.5 32.3 %all-to-all-done.1 = f16[16,64,1024]{2,1,0:T(8,128)(2,1)S(1)} async-done(((f16[16,64,1024]{2,1,0:T(8,128)(2,1)}), f16[16,64,1024]{2,1,0:T(8,128)(2,1)S(1)}, u32[]{:S(2)}, u32[]{:S(2)}) %all-to-all-start.1) | async-done | bytes 2097184 | tf_op jit(solution)/shard_map/all_to_all | solution.py:67
  125.7 0.5 convert_reduce_fusion
  126.2 0.0 copy-done.2
  126.2 0.8 bitcast_add_fusion
  (1 shorter events, 0.0 us)
Async XLA Ops:
  2.9 16.8 %all-to-all-start = ((f16[16,16,256]{2,1,0:T(8,128)(2,1)}), f16[16,16,256]{2,1,0:T(8,128)(2,1)S(1)}, u32[]{:S(2)}, u32[]{:S(2)}) async-start(f16[16,16,256]{2,1,0:T(8,128)(2,1)} %concatenate.9), calls=%async_computation | async-start | bytes 262144 | tf_op jit(solution)/shard_map/all_to_all | solution.py:25
  77.1 2.3 %copy-start = (bf16[1,32,256,128]{3,2,1,0:T(8,128)(2,1)S(1)}, bf16[1,32,256,128]{3,2,1,0:T(8,128)(2,1)}, u32[]{:S(2)}) copy-start(bf16[1,32,256,128]{3,2,1,0:T(8,128)(2,1)} %get-tuple-element.6) | copy-start | bytes 6291460
  82.0 1.0 copy-start.1
  86.0 39.8 %all-to-all-start.1 = ((f16[16,64,1024]{2,1,0:T(8,128)(2,1)}), f16[16,64,1024]{2,1,0:T(8,128)(2,1)S(1)}, u32[]{:S(2)}, u32[]{:S(2)}) async-start(f16[16,64,1024]{2,1,0:T(8,128)(2,1)} %bitcast.61), calls=%async_computation.1 | async-start | bytes 4194304 | tf_op jit(solution)/shard_map/all_to_all | solution.py:67
  92.9 33.4 %copy-start.2 = (f32[1,64,1024]{2,1,0:T(8,128)S(1)}, f32[1,64,1024]{2,1,0:T(8,128)}, u32[]{:S(2)}) copy-start(f32[1,64,1024]{2,1,0:T(8,128)} %param.9) | copy-start | bytes 786436

commit v2 on v1

v2 whole, which is shorter than its diff:
```python
import jax
import jax.numpy as jnp
from jax import lax
from jax.experimental import pallas as pl
from jax.experimental.pallas import tpu as pltpu
from jax.sharding import PartitionSpec as P

TILE = 1024
HALF = 512
UT = 10
LANES = 128
GAIN = 2.0**15
MARK = 16


def gathered(gradient):
    rows, cols = gradient.shape
    n_row = lax.axis_size("row")
    depth = cols // n_row
    out = gradient.T.reshape(n_row, depth, rows)
    got = lax.all_to_all(out, "row", split_axis=0, concat_axis=0, tiled=True)
    narrow = got.reshape(n_row, depth, rows // LANES, LANES).transpose(0, 2, 1, 3).reshape(rows, cols)
    both = jnp.concatenate([gradient, narrow], axis=0).astype(jnp.float32) * GAIN
    every = lax.all_gather(both.astype(jnp.float16), "blk", axis=0, tiled=False)
    return every.astype(jnp.bfloat16)


def product_kernel(jobs, every, out, left_a, left_b, right_a, right_b, sems):
    n_blk = every.shape[0]
    depth = right_a.shape[2]
    unit = depth // n_blk
    wide_a, wide_b = HALF // LANES, TILE // LANES
    share = HALF // (out.shape[0] // 2)

    def place(slot):
        code = jobs[slot]
        within = lax.rem(code, 2 * UT)
        t = within // 2
        i = (t >= 4).astype(jnp.int32) + (t >= 7).astype(jnp.int32) + (t >= 9).astype(jnp.int32)
        j = t - 3 * (t >= 4).astype(jnp.int32) - 2 * (t >= 7).astype(jnp.int32) - (t >= 9).astype(jnp.int32)
        return code < 2 * UT, i * wide_b + lax.rem(within, 2) * wide_a, j * wide_b

    def copies(slot):
        is_left, at_a, at_b = place(slot)
        left = [
            pltpu.make_async_copy(
                every.at[:, pl.ds(pl.multiple_of(depth + unit * at, 16), unit * wide)], dst.at[slot], sems.at[slot, n]
            )
            for n, (at, wide, dst) in enumerate(((at_a, wide_a, left_a), (at_b, wide_b, left_b)))
        ]
        right = [
            pltpu.make_async_copy(every.at[pl.ds(at, wide), pl.ds(0, depth)], dst.at[slot], sems.at[slot, n])
            for n, (at, wide, dst) in enumerate(((at_a, wide_a, right_a), (at_b, wide_b, right_b)))
        ]
        return is_left, left, right

    for slot in range(2):
        is_left, left, right = copies(slot)

        @pl.when(is_left)
        def _():
            for c in left:
                c.start()

        @pl.when(jnp.logical_not(is_left))
        def _():
            for c in right:
                c.start()

    for slot in range(2):
        is_left, left, right = copies(slot)

        @pl.when(is_left)
        def _():
            for c in left:
                c.wait()
            for src, dst, wide in ((left_a, right_a, wide_a), (left_b, right_b, wide_b)):
                for n in range(wide // 2):
                    pair = src[slot, :, 2 * unit * n : 2 * unit * (n + 1), :].astype(jnp.float32)
                    for m in range(2):
                        piece = pair[:, unit * m : unit * (m + 1), :].reshape(depth, LANES)
                        dst[slot, 2 * n + m] = piece.astype(jnp.bfloat16)

        @pl.when(jnp.logical_not(is_left))
        def _():
            for c in right:
                c.wait()

        def top(ref):
            return jnp.max(jnp.abs(ref[slot].astype(jnp.float32)), axis=(0, 1, 2), keepdims=True)[0]

        bound = jnp.maximum(top(right_a), 2.0**-30) * jnp.maximum(top(right_b), 2.0**-30) * (depth / 2.0**15)
        power = jnp.ceil(jnp.log2(bound))
        scale = jnp.exp2(-power)
        for q in range(out.shape[0] // 2):
            out[slot * (out.shape[0] // 2) + q, wide_b * share :, :] = jnp.broadcast_to(power, (MARK, LANES))
        for a in range(wide_a):
            lhs = right_a[slot, a].T
            for b in range(wide_b):
                term = jnp.dot(lhs, right_b[slot, b], preferred_element_type=jnp.float32) * scale
                for m in range(LANES // share):
                    q = slot * (out.shape[0] // 2) + a * (LANES // share) + m
                    out[q, b * share : (b + 1) * share, :] = term[m * share : (m + 1) * share]


def products(jobs, every, n_row):
    depth = every.shape[1] // 2
    n_blk = every.shape[0]
    unit = depth // n_blk
    wide_a, wide_b = HALF // LANES, TILE // LANES
    share = 2 * HALF // n_row
    return pl.pallas_call(
        product_kernel,
        out_shape=jax.ShapeDtypeStruct((n_row, wide_b * share + MARK, LANES), jnp.float32),
        in_specs=[pl.BlockSpec(memory_space=pltpu.SMEM), pl.BlockSpec(memory_space=pl.ANY)],
        out_specs=pl.BlockSpec(memory_space=pltpu.VMEM),
        scratch_shapes=[
            pltpu.VMEM((2, n_blk, unit * wide_a, LANES), jnp.bfloat16),
            pltpu.VMEM((2, n_blk, unit * wide_b, LANES), jnp.bfloat16),
            pltpu.VMEM((2, wide_a, depth, LANES), jnp.bfloat16),
            pltpu.VMEM((2, wide_b, depth, LANES), jnp.bfloat16),
            pltpu.SemaphoreType.DMA((2, 2)),
        ],
        compiler_params=pltpu.CompilerParams(vmem_limit_bytes=24 * 2**20),
        cost_estimate=pl.CostEstimate(
            flops=4 * HALF * TILE * depth, bytes_accessed=every.size, transcendentals=0
        ),
    )(jobs, every)


def per_device(gradient, slot_jobs, old_stats):
    n_row = lax.axis_size("row")
    share = old_stats.shape[1]
    every = gathered(gradient)
    terms = products(slot_jobs[0], every, n_row).astype(jnp.float16)
    got = lax.all_to_all(terms, "row", split_axis=0, concat_axis=0, tiled=True)
    groups = TILE // LANES
    unit = jnp.exp2(got[:, groups * share :, :][:, :1, :1].astype(jnp.float32)) * GAIN**-2
    summed = jnp.sum(got[:, : groups * share].astype(jnp.float32) * unit, axis=0)
    summed = summed.reshape(groups, share, LANES).transpose(1, 0, 2).reshape(share, TILE)
    slot = lax.axis_index("row") // (n_row // 2)
    used = slot_jobs[0, slot] < 4 * UT
    return 0.95 * old_stats + 0.05 * jnp.where(used, summed, 0.0)[None]


def solution(mesh):
    placed = (P("row", "blk"), P("blk", None), P("blk", "row", None))
    return jax.shard_map(
        per_device, mesh=mesh, in_specs=placed, out_specs=P("blk", "row", None), check_vma=False
    )
```

time: 127 us -> 114 us (0.90)
  blocking collectives: 51.3 us -> 65.8 us
  starting transfers between devices: 14.5 us -> 3.85 us
  local copies, waits for them, and re-layouts: 9.73 us -> 1.15 us
  between operations: 8.49 us -> 0.1 us
  other arithmetic: 9.83 us -> 6.48 us
  Pallas kernels: 0 us -> 2.26 us
  waiting for transfers between devices: 32.3 us -> 33.6 us
    all_to_all x0 -> x1, blocking collectives: none -> 13.9 us  [gathered(): got = lax.all_to_all(out, 'row', split_axis=0, concat_axis=0, tiled=True)]
    all_to_all x1 -> x0, starting transfers between devices: 7.58 us -> none  [panels(): lax.all_to_all(jnp.concatenate([out, mark], axis=1), 'row', split_axis=0,...]
    transpose x3 -> x0, other arithmetic: 4.68 us -> none  [the longest x1 3.13 us: panels(): left = left.transpose(1, 0, 2, 3).reshape(n_blk, rows, LANES)]
    transpose x5 -> x0, local copies, waits for them, and re-layouts: 3.82 us -> none  [the longest x1 2.31 us: panels(): left = left.transpose(1, 0, 2, 3).reshape(n_blk, rows, LANES)]
    convert_element_type x1 -> x3, other arithmetic: 0.62 us -> 3.75 us  [the longest x1 1.63 us: per_device(): terms = products(slot_jobs[0], every, n_row).astype(jnp.float16)]
    all_to_all x1, starting transfers between devices: 6.88 us -> 3.85 us  [per_device(): got = lax.all_to_all(terms, 'row', split_axis=0, concat_axis=0, tiled=True)]
    dynamic_slice x2 -> x0, local copies, waits for them, and re-layouts: 2.82 us -> none  [the longest x1 1.42 us: per_device(): used = slot_jobs[0, slot] < 4 * UT]
    pallas_call x0 -> x1, Pallas kernels: none -> 2.26 us  [products(): pl.pallas_call(product_kernel, out_shape=jax.ShapeDtypeStruct((n_row, wid...]
  transfers between devices with their start and end apart: 2 -> 1, of which waited for: 1 -> 1; matrix products, arithmetic and copies ran while one was open for 2% -> 1% of each run, Pallas kernels for 0% -> 0%
where the time goes in v2:
time: 114 us; the launch traced here: 113 us
  blocking collectives  65.8 us (58%)
  waiting for transfers between devices  33.6 us (29%)
  other arithmetic  6.48 us (6%)
  starting transfers between devices  3.85 us (3%)
  Pallas kernels  2.26 us (2%)
  local copies, waits for them, and re-layouts  1.15 us (1%)
    all_gather x1, blocking collectives, gathered(): every = lax.all_gather(both.astype(jnp.float16), 'blk', axis=0, tiled=False)  51.9 us
    all_to_all x1, waiting for transfers between devices, per_device(): got = lax.all_to_all(terms, 'row', split_axis=0, concat_axis=0, tiled=True)  33.6 us
    all_to_all x1, blocking collectives, gathered(): got = lax.all_to_all(out, 'row', split_axis=0, concat_axis=0, tiled=True)  13.9 us
    all_to_all x1, starting transfers between devices, per_device(): got = lax.all_to_all(terms, 'row', split_axis=0, concat_axis=0, tiled=True)  3.85 us
  transfers between devices with their start and end apart: 1, of which 1 were waited for; matrix products, arithmetic and copies ran while one was open for 1% of the time, Pallas kernels for 0%

profile of v2, /device:TPU:1, one launch (start us, length us, event | category | flops | bytes accessed | tf_op | source)
XLA Modules:
  0.0 113.2 jit_solution(5630832660802450076)
XLA Ops:
  0.0 0.9 copy.9
  0.9 13.9 %all_to_all.10 = bf16[16,8,256]{2,1,0:T(8,128)(2,1)S(1)} all-to-all(bf16[16,8,256]{2,1,0:T(8,128)(2,1)S(1)} %bitcast.16), channel_id=1, replica_groups=mesh['row'=16,'blk'=32] {'row'}, dimensions={0} | all-to-all | bytes 131072 | tf_op jit(solution)/shard_map/all_to_all | solution.py:21
  14.8 0.9 multiply_convert_fusion
  15.7 51.9 %all-gather.1 = f16[32,512,128]{2,1,0:T(8,128)(2,1)S(1)} all-gather(f16[1,512,128]{2,1,0:T(8,128)(2,1)S(1)} %multiply_convert_fusion), channel_id=1, replica_groups=mesh['row'=16,'blk'=32] {'blk'}, dimensions={0}, use_global_device_ids=true | all-gather | bytes 4325376 | tf_op jit(solution)/shard_map/all_gather | solution.py:24
  67.6 0.0 copy-start
  67.6 1.2 %convert_element_type.34.every = bf16[32,512,128]{2,1,0:T(8,128)(2,1)S(1)} convert(f16[32,512,128]{2,1,0:T(8,128)(2,1)S(1)} %all-gather.1) | non-fusion elementwise | flops 2097152 | bytes 8388608 | tf_op jit(solution)/shard_map/convert_element_type | solution.py:25
  68.9 0.0 copy-done
  68.9 2.3 %shard_map.37 = f32[16,528,128]{2,1,0:T(8,128)S(1)} custom-call(s32[2]{0:T(128)S(1)} %bitcast.14, bf16[32,512,128]{2,1,0:T(8,128)(2,1)S(1)} %convert_element_type.34.every), custom_call_target="tpu_custom_call" | custom-call | flops 536870912 | bytes 2097152 | tf_op jit(solution)/shard_map/pallas_call | solution.py:112
  71.2 1.6 %convert_element_type.35 = f16[16,528,128]{2,1,0:T(8,128)(2,1)} convert(f32[16,528,128]{2,1,0:T(8,128)S(1)} %shard_map.37) | non-fusion elementwise | flops 1081344 | bytes 6488064 | tf_op jit(solution)/shard_map/convert_element_type | solution.py:135
  72.8 0.0 copy-start.1
  72.8 3.9 %all-to-all-start.1 = ((f16[16,528,128]{2,1,0:T(8,128)(2,1)}), f16[16,528,128]{2,1,0:T(8,128)(2,1)S(1)}, u32[]{:S(2)}, u32[]{:S(2)}) async-start(f16[16,528,128]{2,1,0:T(8,128)(2,1)} %convert_element_type.35), calls=%async_computation.1 | async-start | bytes 4325376 | tf_op jit(solution)/shard_map/all_to_all | solution.py:136
  76.7 0.6 fusion.4
  77.3 33.6 %all-to-all-done.1 = f16[16,528,128]{2,1,0:T(8,128)(2,1)S(1)} async-done(((f16[16,528,128]{2,1,0:T(8,128)(2,1)}), f16[16,528,128]{2,1,0:T(8,128)(2,1)S(1)}, u32[]{:S(2)}, u32[]{:S(2)}) %all-to-all-start.1) | async-done | bytes 2162720 | tf_op jit(solution)/shard_map/all_to_all | solution.py:136
  110.9 0.2 fusion.3
  111.1 0.5 multiply_reduce_fusion
  111.6 0.7 select_multiply_fusion
  112.3 0.2 copy.10
  112.5 0.0 copy-done.1
  112.5 0.7 multiply_add_fusion
  (1 shorter events, 0.0 us)
Async XLA Ops:
  67.6 1.3 %copy-start = (s32[1,2]{1,0:T(1,128)S(1)}, s32[1,2]{1,0:T(1,128)}, u32[]{:S(2)}) copy-start(s32[1,2]{1,0:T(1,128)} %param.4) | copy-start | bytes 28
  72.8 39.7 %copy-start.1 = (f32[1,64,1024]{2,1,0:T(8,128)S(1)}, f32[1,64,1024]{2,1,0:T(8,128)}, u32[]{:S(2)}) copy-start(f32[1,64,1024]{2,1,0:T(8,128)} %param.5) | copy-start | bytes 786436
  72.8 38.1 %all-to-all-start.1 = ((f16[16,528,128]{2,1,0:T(8,128)(2,1)}), f16[16,528,128]{2,1,0:T(8,128)(2,1)S(1)}, u32[]{:S(2)}, u32[]{:S(2)}) async-start(f16[16,528,128]{2,1,0:T(8,128)(2,1)} %convert_element_type.35), calls=%async_computation.1 | async-start | bytes 4325376 | tf_op jit(solution)/shard_map/all_to_all | solution.py:136

commit v3 on v2

--- a/solution.py
+++ b/solution.py
@@ -10,7 +10,7 @@
 UT = 10
 LANES = 128
 GAIN = 2.0**15
-MARK = 16
+MARK = 8
 
 
 def gathered(gradient):
@@ -91,7 +91,7 @@
 
         bound = jnp.maximum(top(right_a), 2.0**-30) * jnp.maximum(top(right_b), 2.0**-30) * (depth / 2.0**15)
         power = jnp.ceil(jnp.log2(bound))
-        scale = jnp.exp2(-power)
+        scale = jnp.where(jobs[slot] < 4 * UT, jnp.exp2(-power), 0.0)
         for q in range(out.shape[0] // 2):
             out[slot * (out.shape[0] // 2) + q, wide_b * share :, :] = jnp.broadcast_to(power, (MARK, LANES))
         for a in range(wide_a):
@@ -135,12 +135,10 @@
     terms = products(slot_jobs[0], every, n_row).astype(jnp.float16)
     got = lax.all_to_all(terms, "row", split_axis=0, concat_axis=0, tiled=True)
     groups = TILE // LANES
-    unit = jnp.exp2(got[:, groups * share :, :][:, :1, :1].astype(jnp.float32)) * GAIN**-2
+    unit = jnp.exp2(got[:, groups * share :, :][:, :1, :1].astype(jnp.float32)) * (0.05 * GAIN**-2)
     summed = jnp.sum(got[:, : groups * share].astype(jnp.float32) * unit, axis=0)
     summed = summed.reshape(groups, share, LANES).transpose(1, 0, 2).reshape(share, TILE)
-    slot = lax.axis_index("row") // (n_row // 2)
-    used = slot_jobs[0, slot] < 4 * UT
-    return 0.95 * old_stats + 0.05 * jnp.where(used, summed, 0.0)[None]
+    return 0.95 * old_stats + summed[None]
 
 
 def solution(mesh):

time: 114 us -> 105 us (0.921)
  waiting for transfers between devices: 33.6 us -> 0 us
  blocking collectives: 65.8 us -> 97.5 us
  starting transfers between devices: 3.85 us -> 0 us
  other arithmetic: 6.48 us -> 3.46 us
    all_to_all x1 -> x0, waiting for transfers between devices: 33.6 us -> none  [per_device(): got = lax.all_to_all(terms, 'row', split_axis=0, concat_axis=0, tiled=True)]
    all_to_all x0 -> x1, blocking collectives: none -> 31.7 us  [per_device(): got = lax.all_to_all(terms, 'row', split_axis=0, concat_axis=0, tiled=True)]
    all_to_all x1 -> x0, starting transfers between devices: 3.85 us -> none  [per_device(): got = lax.all_to_all(terms, 'row', split_axis=0, concat_axis=0, tiled=True)]
    convert_element_type x1, other arithmetic: 1.63 us -> 0.28 us  [per_device(): terms = products(slot_jobs[0], every, n_row).astype(jnp.float16)]
  transfers between devices with their start and end apart: 1 -> 0, of which waited for: 1 -> 0; matrix products, arithmetic and copies ran while one was open for 1% -> 0% of each run, Pallas kernels for 0% -> 0%
where the time goes in v3:
time: 105 us
  blocking collectives  97.5 us (93%)
  other arithmetic  3.46 us (3%)
  Pallas kernels  2.39 us (2%)
  local copies, waits for them, and re-layouts  1.15 us (1%)
    all_gather x1, blocking collectives, gathered(): every = lax.all_gather(both.astype(jnp.float16), 'blk', axis=0, tiled=False)  51.9 us
    all_to_all x1, blocking collectives, per_device(): got = lax.all_to_all(terms, 'row', split_axis=0, concat_axis=0, tiled=True)  31.7 us
    all_to_all x1, blocking collectives, gathered(): got = lax.all_to_all(out, 'row', split_axis=0, concat_axis=0, tiled=True)  13.9 us
    pallas_call x1, Pallas kernels, products(): pl.pallas_call(product_kernel, out_shape=jax.ShapeDtypeStruct((n_row, wid...  2.39 us

profile of v3, /device:TPU:1, one launch (start us, length us, event | category | flops | bytes accessed | tf_op | source)
XLA Modules:
  0.0 104.6 jit_solution(7166404846577854967)
XLA Ops:
  0.0 0.9 copy.9
  0.9 13.9 %all_to_all.10 = bf16[16,8,256]{2,1,0:T(8,128)(2,1)S(1)} all-to-all(bf16[16,8,256]{2,1,0:T(8,128)(2,1)S(1)} %bitcast.15), channel_id=1, replica_groups=mesh['row'=16,'blk'=32] {'row'}, dimensions={0} | all-to-all | bytes 131072 | tf_op jit(solution)/shard_map/all_to_all | solution.py:21
  14.8 0.9 multiply_convert_fusion
  15.7 51.9 %all-gather.1 = f16[32,512,128]{2,1,0:T(8,128)(2,1)S(1)} all-gather(f16[1,512,128]{2,1,0:T(8,128)(2,1)S(1)} %multiply_convert_fusion), channel_id=1, replica_groups=mesh['row'=16,'blk'=32] {'blk'}, dimensions={0}, use_global_device_ids=true | all-gather | bytes 4325376 | tf_op jit(solution)/shard_map/all_gather | solution.py:24
  67.6 0.0 copy-start
  67.6 0.8 convert_element_type.34.every
  68.5 0.0 copy-done
  68.5 2.4 %shard_map.37 = f32[16,520,128]{2,1,0:T(8,128)S(1)} custom-call(s32[2]{0:T(128)S(1)} %bitcast.13, bf16[32,512,128]{2,1,0:T(8,128)(2,1)S(1)} %convert_element_type.34.every), custom_call_target="tpu_custom_call" | custom-call | flops 536870912 | bytes 2097152 | tf_op jit(solution)/shard_map/pallas_call | solution.py:112
  70.9 0.3 convert_element_type.35
  71.2 0.0 copy-start.1
  71.2 31.7 %all_to_all.11 = f16[16,520,128]{2,1,0:T(8,128)(2,1)S(1)} all-to-all(f16[16,520,128]{2,1,0:T(8,128)(2,1)S(1)} %convert_element_type.35), channel_id=1, replica_groups=mesh['row'=16,'blk'=32] {'row'}, dimensions={0} | all-to-all | bytes 4259840 | tf_op jit(solution)/shard_map/all_to_all | solution.py:136
  102.9 0.2 fusion.3
  103.1 0.5 multiply_reduce_fusion
  103.6 0.2 copy.10
  103.8 0.0 copy-done.1
  103.9 0.7 multiply_add_fusion
  (1 shorter events, 0.0 us)
Async XLA Ops:
  67.6 0.9 copy-start
  71.2 32.7 %copy-start.1 = (f32[1,64,1024]{2,1,0:T(8,128)S(1)}, f32[1,64,1024]{2,1,0:T(8,128)}, u32[]{:S(2)}) copy-start(f32[1,64,1024]{2,1,0:T(8,128)} %param.5) | copy-start | bytes 786436

commit v4 on v3

--- a/solution.py
+++ b/solution.py
@@ -1,3 +1,5 @@
+import math
+
 import jax
 import jax.numpy as jnp
 from jax import lax
@@ -30,7 +32,14 @@
     depth = right_a.shape[2]
     unit = depth // n_blk
     wide_a, wide_b = HALF // LANES, TILE // LANES
-    share = HALF // (out.shape[0] // 2)
+    n_row = out.shape[0]
+    share = HALF // (n_row // 2)
+    side = math.isqrt(n_row)
+    along_x = lax.rem(lax.axis_index("blk"), 2) == 0
+    fraction = lax.axis_index("row").astype(jnp.float32) / n_row
+
+    def chunk(row):
+        return jnp.where(along_x, row % side * side + row // side, row)
 
     def place(slot):
         code = jobs[slot]
@@ -87,20 +96,23 @@
                 c.wait()
 
         def top(ref):
-            return jnp.max(jnp.abs(ref[slot].astype(jnp.float32)), axis=(0, 1, 2), keepdims=True)[0]
+            most = jnp.max(jnp.abs(ref[slot]), axis=0).astype(jnp.float32)
+            return jnp.max(most, axis=(0, 1), keepdims=True)
 
         bound = jnp.maximum(top(right_a), 2.0**-30) * jnp.maximum(top(right_b), 2.0**-30) * (depth / 2.0**15)
-        power = jnp.ceil(jnp.log2(bound))
+        power = jnp.ceil(jnp.log2(bound)) + fraction
         scale = jnp.where(jobs[slot] < 4 * UT, jnp.exp2(-power), 0.0)
-        for q in range(out.shape[0] // 2):
-            out[slot * (out.shape[0] // 2) + q, wide_b * share :, :] = jnp.broadcast_to(power, (MARK, LANES))
-        for a in range(wide_a):
-            lhs = right_a[slot, a].T
-            for b in range(wide_b):
-                term = jnp.dot(lhs, right_b[slot, b], preferred_element_type=jnp.float32) * scale
-                for m in range(LANES // share):
-                    q = slot * (out.shape[0] // 2) + a * (LANES // share) + m
-                    out[q, b * share : (b + 1) * share, :] = term[m * share : (m + 1) * share]
+        places = [chunk(slot * (n_row // 2) + q) for q in range(n_row // 2)]
+        for to in places:
+            out[to, wide_b * share :, :] = jnp.broadcast_to(power, (MARK, LANES))
+        lhs = jnp.concatenate([right_a[slot, a].T for a in range(wide_a)], axis=0)
+        for b in range(0, wide_b, 2):
+            rhs = jnp.concatenate([right_b[slot, b], right_b[slot, b + 1]], axis=1)
+            term = jnp.dot(lhs, rhs, preferred_element_type=jnp.float32) * scale
+            for n in range(2):
+                for q, to in enumerate(places):
+                    piece = term[q * share : (q + 1) * share, n * LANES : (n + 1) * LANES]
+                    out[to, (b + n) * share : (b + n + 1) * share, :] = piece
 
 
 def products(jobs, every, n_row):
@@ -128,15 +140,39 @@
     )(jobs, every)
 
 
+def steps(n_row, n_blk):
+    side = math.isqrt(n_row)
+    along_x = [[y * side + x for x in range(side)] for y in range(side)]
+    along_y = [[y * side + x for y in range(side)] for x in range(side)]
+    return [
+        [[row * n_blk + b for row in line] for b in range(n_blk) for line in (lines if b % 2 == 0 else others)]
+        for lines, others in ((along_x, along_y), (along_y, along_x))
+    ]
+
+
 def per_device(gradient, slot_jobs, old_stats):
-    n_row = lax.axis_size("row")
+    n_row, n_blk = lax.axis_size("row"), lax.axis_size("blk")
+    side = math.isqrt(n_row)
     share = old_stats.shape[1]
+    groups = TILE // LANES
+    body = groups * share
+    first, second = steps(n_row, n_blk)
+
+    def exchange(terms, lines):
+        return lax.all_to_all(
+            terms, ("row", "blk"), split_axis=0, concat_axis=0, axis_index_groups=lines, tiled=True
+        )
+
     every = gathered(gradient)
     terms = products(slot_jobs[0], every, n_row).astype(jnp.float16)
-    got = lax.all_to_all(terms, "row", split_axis=0, concat_axis=0, tiled=True)
-    groups = TILE // LANES
-    unit = jnp.exp2(got[:, groups * share :, :][:, :1, :1].astype(jnp.float32)) * (0.05 * GAIN**-2)
-    summed = jnp.sum(got[:, : groups * share].astype(jnp.float32) * unit, axis=0)
+    got = exchange(terms.reshape(side, side, body + MARK, LANES), first)
+    power = got[:, :, body:].astype(jnp.float32)
+    top = jnp.max(power, axis=0) + 2.0
+    factor = jnp.exp2(power - top)[:, :, :1, :1]
+    summed = jnp.sum(got[:, :, :body].astype(jnp.float32) * factor, axis=0)
+    got = exchange(jnp.concatenate([summed, top], axis=1).astype(jnp.float16), second)
+    unit = jnp.exp2(got[:, body:][:, :1, :1].astype(jnp.float32)) * (0.05 * GAIN**-2)
+    summed = jnp.sum(got[:, :body].astype(jnp.float32) * unit, axis=0)
     summed = summed.reshape(groups, share, LANES).transpose(1, 0, 2).reshape(share, TILE)
     return 0.95 * old_stats + summed[None]
 

time: 105 us -> 102 us (0.971)
  blocking collectives: 97.5 us -> 93.5 us
    all_to_all x1 -> x2, blocking collectives: 31.7 us -> 27.7 us  [exchange(): lax.all_to_all(terms, ('row', 'blk'), split_axis=0, concat_axis=0, axis_i...]
where the time goes in v4:
time: 102 us; the launch traced here: 101 us
  blocking collectives  93.5 us (92%)
  other arithmetic  4.02 us (4%)
  Pallas kernels  2.49 us (2%)
  local copies, waits for them, and re-layouts  1.15 us (1%)
    all_gather x1, blocking collectives, gathered(): every = lax.all_gather(both.astype(jnp.float16), 'blk', axis=0, tiled=False)  51.9 us
    all_to_all x2, blocking collectives, exchange(): lax.all_to_all(terms, ('row', 'blk'), split_axis=0, concat_axis=0, axis_i...  27.7 us
    all_to_all x1, blocking collectives, gathered(): got = lax.all_to_all(out, 'row', split_axis=0, concat_axis=0, tiled=True)  13.9 us
    pallas_call x1, Pallas kernels, products(): pl.pallas_call(product_kernel, out_shape=jax.ShapeDtypeStruct((n_row, wid...  2.49 us

profile of v4, /device:TPU:1, one launch (start us, length us, event | category | flops | bytes accessed | tf_op | source)
XLA Modules:
  0.0 101.3 jit_solution(5956551434280614512)
XLA Ops:
  0.0 0.9 copy.12
  0.9 13.9 %all_to_all.15 = bf16[16,8,256]{2,1,0:T(8,128)(2,1)S(1)} all-to-all(bf16[16,8,256]{2,1,0:T(8,128)(2,1)S(1)} %bitcast.17), channel_id=1, replica_groups=mesh['row'=16,'blk'=32] {'row'}, dimensions={0} | all-to-all | bytes 131072 | tf_op jit(solution)/shard_map/all_to_all | solution.py:23
  14.8 0.9 multiply_convert_fusion
  15.7 51.9 %all-gather.1 = f16[32,512,128]{2,1,0:T(8,128)(2,1)S(1)} all-gather(f16[1,512,128]{2,1,0:T(8,128)(2,1)S(1)} %multiply_convert_fusion), channel_id=1, replica_groups=mesh['row'=16,'blk'=32] {'blk'}, dimensions={0}, use_global_device_ids=true | all-gather | bytes 4325376 | tf_op jit(solution)/shard_map/all_gather | solution.py:26
  67.6 0.0 copy-start
  67.6 0.8 convert_element_type.41.every
  68.5 0.0 copy-done
  68.5 2.5 %shard_map.37 = f32[16,520,128]{2,1,0:T(8,128)S(1)} custom-call(s32[2]{0:T(128)S(1)} %bitcast.14, bf16[32,512,128]{2,1,0:T(8,128)(2,1)S(1)} %convert_element_type.41.every), custom_call_target="tpu_custom_call" | custom-call | flops 536870912 | bytes 2097152 | tf_op jit(solution)/shard_map/pallas_call | solution.py:124
  71.0 0.3 convert_element_type.42
  71.3 18.3 %all_to_all.16 = f16[4,4,520,128]{3,2,1,0:T(8,128)(2,1)S(1)} all-to-all(f16[4,4,520,128]{3,2,1,0:T(8,128)(2,1)S(1)} %bitcast.15), channel_id=1, replica_groups={{0,32,64,96},{128,160,192,224},{256,288,320,352},{384,416,448,480},{1,1..., dimensions={0} | all-to-all | bytes 4259840 | tf_op jit(solution)/shard_map/all_to_all | solution.py:162
  89.6 0.1 fusion.3
  89.7 0.0 copy-start.1
  89.7 0.6 multiply_reduce_fusion
  90.3 0.1 convert.6
  90.4 0.1 pad_maximum_fusion
  90.6 9.4 %all_to_all.17 = f16[4,520,128]{2,1,0:T(8,128)(2,1)S(1)} all-to-all(f16[4,520,128]{2,1,0:T(8,128)(2,1)S(1)} %pad_maximum_fusion), channel_id=1, replica_groups={{0,128,256,384},{32,160,288,416},{64,192,320,448},{96,224,352,480},{1,3..., dimensions={0} | all-to-all | bytes 1064960 | tf_op jit(solution)/shard_map/all_to_all | solution.py:162
  100.0 0.1 fusion.7
  100.1 0.2 multiply_reduce_fusion.1
  100.3 0.2 copy.13
  100.5 0.0 copy-done.1
  100.5 0.7 multiply_add_fusion
  (5 shorter events, 0.1 us)
Async XLA Ops:
  67.6 0.9 copy-start
  89.7 10.8 %copy-start.1 = (f32[1,64,1024]{2,1,0:T(8,128)S(1)}, f32[1,64,1024]{2,1,0:T(8,128)}, u32[]{:S(2)}) copy-start(f32[1,64,1024]{2,1,0:T(8,128)} %param.5) | copy-start | bytes 786436

commit v5 on v4

--- a/solution.py
+++ b/solution.py
@@ -95,23 +95,25 @@
             for c in right:
                 c.wait()
 
-        def top(ref):
-            most = jnp.max(jnp.abs(ref[slot]), axis=0).astype(jnp.float32)
-            return jnp.max(most, axis=(0, 1), keepdims=True)
+    def top(ref, slot):
+        most = jnp.max(jnp.abs(ref[slot]), axis=0).astype(jnp.float32)
+        return jnp.max(most, axis=(0, 1), keepdims=True)
 
-        bound = jnp.maximum(top(right_a), 2.0**-30) * jnp.maximum(top(right_b), 2.0**-30) * (depth / 2.0**15)
-        power = jnp.ceil(jnp.log2(bound)) + fraction
-        scale = jnp.where(jobs[slot] < 4 * UT, jnp.exp2(-power), 0.0)
+    tilt = lax.broadcasted_iota(jnp.int32, (MARK // 2, LANES), 1).astype(jnp.float32) / LANES
+    for slot in range(2):
+        bound = jnp.maximum(top(right_a, slot), 2.0**-30) * jnp.maximum(top(right_b, slot), 2.0**-30)
+        power = jnp.ceil(jnp.log2(bound * (depth / 2.0**14))) + fraction
+        scale = jnp.where(jobs[slot] < 4 * UT, jnp.exp2(tilt[:1] - power), 0.0)
         places = [chunk(slot * (n_row // 2) + q) for q in range(n_row // 2)]
         for to in places:
-            out[to, wide_b * share :, :] = jnp.broadcast_to(power, (MARK, LANES))
+            out[to, wide_b * share :, :] = jnp.concatenate([jnp.broadcast_to(power, tilt.shape), tilt], axis=0)
         lhs = jnp.concatenate([right_a[slot, a].T for a in range(wide_a)], axis=0)
         for b in range(0, wide_b, 2):
             rhs = jnp.concatenate([right_b[slot, b], right_b[slot, b + 1]], axis=1)
-            term = jnp.dot(lhs, rhs, preferred_element_type=jnp.float32) * scale
+            term = jnp.dot(lhs, rhs, preferred_element_type=jnp.float32)
             for n in range(2):
                 for q, to in enumerate(places):
-                    piece = term[q * share : (q + 1) * share, n * LANES : (n + 1) * LANES]
+                    piece = term[q * share : (q + 1) * share, n * LANES : (n + 1) * LANES] * scale
                     out[to, (b + n) * share : (b + n + 1) * share, :] = piece
 
 
@@ -171,7 +173,8 @@
     factor = jnp.exp2(power - top)[:, :, :1, :1]
     summed = jnp.sum(got[:, :, :body].astype(jnp.float32) * factor, axis=0)
     got = exchange(jnp.concatenate([summed, top], axis=1).astype(jnp.float16), second)
-    unit = jnp.exp2(got[:, body:][:, :1, :1].astype(jnp.float32)) * (0.05 * GAIN**-2)
+    mark = got[:, body:].astype(jnp.float32)
+    unit = jnp.exp2(mark[:, :1] - mark[:, -1:]) * (4.0 * 0.05 * GAIN**-2)
     summed = jnp.sum(got[:, :body].astype(jnp.float32) * unit, axis=0)
     summed = summed.reshape(groups, share, LANES).transpose(1, 0, 2).reshape(share, TILE)
     return 0.95 * old_stats + summed[None]

time: 102 us -> 101 us (level)
  no operation moved by 1% of the time
where the time goes in v5:
time: 101 us
  blocking collectives  93.6 us (93%)
  other arithmetic  3.81 us (4%)
  Pallas kernels  2.16 us (2%)
  local copies, waits for them, and re-layouts  1.15 us (1%)
    all_gather x1, blocking collectives, gathered(): every = lax.all_gather(both.astype(jnp.float16), 'blk', axis=0, tiled=False)  51.9 us
    all_to_all x2, blocking collectives, exchange(): lax.all_to_all(terms, ('row', 'blk'), split_axis=0, concat_axis=0, axis_i...  27.8 us
    all_to_all x1, blocking collectives, gathered(): got = lax.all_to_all(out, 'row', split_axis=0, concat_axis=0, tiled=True)  13.9 us
    pallas_call x1, Pallas kernels, products(): pl.pallas_call(product_kernel, out_shape=jax.ShapeDtypeStruct((n_row, wid...  2.16 us

profile of v5, /device:TPU:1, one launch (start us, length us, event | category | flops | bytes accessed | tf_op | source)
XLA Modules:
  0.0 100.9 jit_solution(17776685944615072187)
XLA Ops:
  0.0 0.9 copy.31
  0.9 13.9 %all_to_all.15 = bf16[16,8,256]{2,1,0:T(8,128)(2,1)S(1)} all-to-all(bf16[16,8,256]{2,1,0:T(8,128)(2,1)S(1)} %bitcast.18), channel_id=1, replica_groups=mesh['row'=16,'blk'=32] {'row'}, dimensions={0} | all-to-all | bytes 131072 | tf_op jit(solution)/shard_map/all_to_all | solution.py:23
  14.8 0.9 multiply_convert_fusion
  15.7 51.9 %all-gather.1 = f16[32,512,128]{2,1,0:T(8,128)(2,1)S(1)} all-gather(f16[1,512,128]{2,1,0:T(8,128)(2,1)S(1)} %multiply_convert_fusion), channel_id=1, replica_groups=mesh['row'=16,'blk'=32] {'blk'}, dimensions={0}, use_global_device_ids=true | all-gather | bytes 4325376 | tf_op jit(solution)/shard_map/all_gather | solution.py:26
  67.6 0.0 copy-start
  67.6 0.8 convert_element_type.41.every
  68.5 0.0 copy-done
  68.5 2.2 %shard_map.37 = f32[16,520,128]{2,1,0:T(8,128)S(1)} custom-call(s32[2]{0:T(128)S(1)} %bitcast.15, bf16[32,512,128]{2,1,0:T(8,128)(2,1)S(1)} %convert_element_type.41.every), custom_call_target="tpu_custom_call" | custom-call | flops 536870912 | bytes 2097152 | tf_op jit(solution)/shard_map/pallas_call | solution.py:126
  70.7 0.3 convert_element_type.42
  70.9 18.1 %all_to_all.16 = f16[4,4,520,128]{3,2,1,0:T(8,128)(2,1)S(1)} all-to-all(f16[4,4,520,128]{3,2,1,0:T(8,128)(2,1)S(1)} %bitcast.16), channel_id=1, replica_groups={{0,32,64,96},{128,160,192,224},{256,288,320,352},{384,416,448,480},{1,1..., dimensions={0} | all-to-all | bytes 4259840 | tf_op jit(solution)/shard_map/all_to_all | solution.py:164
  89.1 0.1 fusion.3
  89.3 0.0 copy-start.1
  89.3 0.6 multiply_reduce_fusion
  89.9 0.1 convert.6
  89.9 0.1 pad_maximum_fusion
  90.1 9.7 %all_to_all.17 = f16[4,520,128]{2,1,0:T(8,128)(2,1)S(1)} all-to-all(f16[4,520,128]{2,1,0:T(8,128)(2,1)S(1)} %pad_maximum_fusion), channel_id=1, replica_groups={{0,128,256,384},{32,160,288,416},{64,192,320,448},{96,224,352,480},{1,3..., dimensions={0} | all-to-all | bytes 1064960 | tf_op jit(solution)/shard_map/all_to_all | solution.py:164
  99.8 0.1 multiply_reduce_fusion.1
  99.9 0.2 copy.34
  100.1 0.0 copy-done.1
  100.1 0.7 multiply_add_fusion
  (7 shorter events, 0.1 us)
Async XLA Ops:
  67.6 0.9 copy-start
  89.3 10.9 %copy-start.1 = (f32[1,64,1024]{2,1,0:T(8,128)S(1)}, f32[1,64,1024]{2,1,0:T(8,128)}, u32[]{:S(2)}) copy-start(f32[1,64,1024]{2,1,0:T(8,128)} %param.5) | copy-start | bytes 786436

commit v6 on v5

--- a/solution.py
+++ b/solution.py
@@ -3,6 +3,7 @@
 import jax
 import jax.numpy as jnp
 from jax import lax
+from jax.experimental.layout import Layout, with_layout_constraint
 from jax.experimental import pallas as pl
 from jax.experimental.pallas import tpu as pltpu
 from jax.sharding import PartitionSpec as P
@@ -19,15 +20,16 @@
     rows, cols = gradient.shape
     n_row = lax.axis_size("row")
     depth = cols // n_row
-    out = gradient.T.reshape(n_row, depth, rows)
+    scaled = lax.optimization_barrier((gradient.astype(jnp.float32) * GAIN).astype(jnp.float16))
+    out = scaled.T.reshape(n_row, depth, rows)
     got = lax.all_to_all(out, "row", split_axis=0, concat_axis=0, tiled=True)
     narrow = got.reshape(n_row, depth, rows // LANES, LANES).transpose(0, 2, 1, 3).reshape(rows, cols)
-    both = jnp.concatenate([gradient, narrow], axis=0).astype(jnp.float32) * GAIN
-    every = lax.all_gather(both.astype(jnp.float16), "blk", axis=0, tiled=False)
+    both = with_layout_constraint(jnp.concatenate([scaled, narrow], axis=0), Layout(major_to_minor=(0, 1)))
+    every = lax.all_gather(both, "blk", axis=0, tiled=False)
     return every.astype(jnp.bfloat16)
 
 
-def product_kernel(jobs, every, out, left_a, left_b, right_a, right_b, sems):
+def product_kernel(jobs, every, out, right_a, right_b):
     n_blk = every.shape[0]
     depth = right_a.shape[2]
     unit = depth // n_blk
@@ -49,51 +51,25 @@
         j = t - 3 * (t >= 4).astype(jnp.int32) - 2 * (t >= 7).astype(jnp.int32) - (t >= 9).astype(jnp.int32)
         return code < 2 * UT, i * wide_b + lax.rem(within, 2) * wide_a, j * wide_b
 
-    def copies(slot):
+    for slot in range(2):
         is_left, at_a, at_b = place(slot)
-        left = [
-            pltpu.make_async_copy(
-                every.at[:, pl.ds(pl.multiple_of(depth + unit * at, 16), unit * wide)], dst.at[slot], sems.at[slot, n]
-            )
-            for n, (at, wide, dst) in enumerate(((at_a, wide_a, left_a), (at_b, wide_b, left_b)))
-        ]
-        right = [
-            pltpu.make_async_copy(every.at[pl.ds(at, wide), pl.ds(0, depth)], dst.at[slot], sems.at[slot, n])
-            for n, (at, wide, dst) in enumerate(((at_a, wide_a, right_a), (at_b, wide_b, right_b)))
-        ]
-        return is_left, left, right
-
-    for slot in range(2):
-        is_left, left, right = copies(slot)
+        panels = ((at_a, wide_a, right_a), (at_b, wide_b, right_b))
 
         @pl.when(is_left)
         def _():
-            for c in left:
-                c.start()
-
-        @pl.when(jnp.logical_not(is_left))
-        def _():
-            for c in right:
-                c.start()
-
-    for slot in range(2):
-        is_left, left, right = copies(slot)
-
-        @pl.when(is_left)
-        def _():
-            for c in left:
-                c.wait()
-            for src, dst, wide in ((left_a, right_a, wide_a), (left_b, right_b, wide_b)):
+            for at, wide, dst in panels:
                 for n in range(wide // 2):
-                    pair = src[slot, :, 2 * unit * n : 2 * unit * (n + 1), :].astype(jnp.float32)
+                    from_row = pl.multiple_of(depth + unit * at, 2 * unit) + 2 * unit * n
+                    pair = every[:, pl.ds(from_row, 2 * unit), :].astype(jnp.float32)
                     for m in range(2):
                         piece = pair[:, unit * m : unit * (m + 1), :].reshape(depth, LANES)
                         dst[slot, 2 * n + m] = piece.astype(jnp.bfloat16)
 
         @pl.when(jnp.logical_not(is_left))
         def _():
-            for c in right:
-                c.wait()
+            for at, wide, dst in panels:
+                for n in range(wide):
+                    dst[slot, n] = every[at + n, :depth, :]
 
     def top(ref, slot):
         most = jnp.max(jnp.abs(ref[slot]), axis=0).astype(jnp.float32)
@@ -126,14 +102,11 @@
     return pl.pallas_call(
         product_kernel,
         out_shape=jax.ShapeDtypeStruct((n_row, wide_b * share + MARK, LANES), jnp.float32),
-        in_specs=[pl.BlockSpec(memory_space=pltpu.SMEM), pl.BlockSpec(memory_space=pl.ANY)],
+        in_specs=[pl.BlockSpec(memory_space=pltpu.SMEM), pl.BlockSpec(memory_space=pltpu.VMEM)],
         out_specs=pl.BlockSpec(memory_space=pltpu.VMEM),
         scratch_shapes=[
-            pltpu.VMEM((2, n_blk, unit * wide_a, LANES), jnp.bfloat16),
-            pltpu.VMEM((2, n_blk, unit * wide_b, LANES), jnp.bfloat16),
             pltpu.VMEM((2, wide_a, depth, LANES), jnp.bfloat16),
             pltpu.VMEM((2, wide_b, depth, LANES), jnp.bfloat16),
-            pltpu.SemaphoreType.DMA((2, 2)),
         ],
         compiler_params=pltpu.CompilerParams(vmem_limit_bytes=24 * 2**20),
         cost_estimate=pl.CostEstimate(

time: 101 us -> 100 us (0.990)
  no operation moved by 1% of the time
where the time goes in v6:
time: 100 us; the launch traced here: 99.9 us
  blocking collectives  93.7 us (94%)
  other arithmetic  3.47 us (3%)
  Pallas kernels  2.18 us (2%)
    all_gather x1, blocking collectives, gathered(): every = lax.all_gather(both, 'blk', axis=0, tiled=False)  51.9 us
    all_to_all x2, blocking collectives, exchange(): lax.all_to_all(terms, ('row', 'blk'), split_axis=0, concat_axis=0, axis_i...  27.9 us
    all_to_all x1, blocking collectives, gathered(): got = lax.all_to_all(out, 'row', split_axis=0, concat_axis=0, tiled=True)  13.9 us
    pallas_call x1, Pallas kernels, products(): pl.pallas_call(product_kernel, out_shape=jax.ShapeDtypeStruct((n_row, wid...  2.18 us

profile of v6, /device:TPU:1, one launch (start us, length us, event | category | flops | bytes accessed | tf_op | source)
XLA Modules:
  0.0 99.9 jit_solution(8872558343142364258)
XLA Ops:
  0.0 0.9 multiply_convert_fusion
  0.9 0.1 copy.31
  1.0 13.9 %all_to_all.15 = f16[16,8,256]{2,1,0:T(8,128)(2,1)S(1)} all-to-all(f16[16,8,256]{2,1,0:T(8,128)(2,1)S(1)} %bitcast.19), channel_id=1, replica_groups=mesh['row'=16,'blk'=32] {'row'}, dimensions={0} | all-to-all | bytes 131072 | tf_op jit(solution)/shard_map/all_to_all | solution.py:25
  14.9 51.9 %all-gather.2 = f16[16384,128]{1,0:T(8,128)(2,1)S(1)} all-gather(f16[512,128]{1,0:T(8,128)(2,1)S(1)} %pad_maximum_fusion.1), channel_id=2, replica_groups=mesh['row'=16,'blk'=32] {'blk'}, dimensions={0}, use_global_device_ids=true | all-gather | bytes 4325376 | tf_op jit(solution)/shard_map/all_gather | solution.py:28
  66.8 0.0 copy-start
  66.8 0.5 convert_element_type.33
  67.3 0.2 copy-done
  67.5 2.2 %shard_map.37 = f32[16,520,128]{2,1,0:T(8,128)S(1)} custom-call(s32[2]{0:T(128)S(1)} %bitcast.15, bf16[32,512,128]{2,1,0:T(8,128)(2,1)S(1)} %bitcast.14), custom_call_target="tpu_custom_call" | custom-call | flops 536870912 | bytes 2097152 | tf_op jit(solution)/shard_map/pallas_call | solution.py:102
  69.7 0.3 convert_element_type.28
  70.0 18.3 %all_to_all.16 = f16[4,4,520,128]{3,2,1,0:T(8,128)(2,1)S(1)} all-to-all(f16[4,4,520,128]{3,2,1,0:T(8,128)(2,1)S(1)} %bitcast.16), channel_id=1, replica_groups={{0,32,64,96},{128,160,192,224},{256,288,320,352},{384,416,448,480},{1,1..., dimensions={0} | all-to-all | bytes 4259840 | tf_op jit(solution)/shard_map/all_to_all | solution.py:137
  88.3 0.1 fusion.3
  88.4 0.0 copy-start.1
  88.4 0.6 multiply_reduce_fusion
  89.0 0.1 convert.6
  89.1 0.1 pad_maximum_fusion
  89.3 9.6 %all_to_all.17 = f16[4,520,128]{2,1,0:T(8,128)(2,1)S(1)} all-to-all(f16[4,520,128]{2,1,0:T(8,128)(2,1)S(1)} %pad_maximum_fusion), channel_id=1, replica_groups={{0,128,256,384},{32,160,288,416},{64,192,320,448},{96,224,352,480},{1,3..., dimensions={0} | all-to-all | bytes 1064960 | tf_op jit(solution)/shard_map/all_to_all | solution.py:137
  98.9 0.1 multiply_reduce_fusion.1
  99.0 0.2 copy.34
  99.2 0.0 copy-done.1
  99.2 0.7 multiply_add_fusion
  (8 shorter events, 0.1 us)
Async XLA Ops:
  66.8 0.7 copy-start
  88.4 10.8 %copy-start.1 = (f32[1,64,1024]{2,1,0:T(8,128)S(1)}, f32[1,64,1024]{2,1,0:T(8,128)}, u32[]{:S(2)}) copy-start(f32[1,64,1024]{2,1,0:T(8,128)} %param.5) | copy-start | bytes 786436

commit v7 on v6

--- a/solution.py
+++ b/solution.py
@@ -29,7 +29,7 @@
     return every.astype(jnp.bfloat16)
 
 
-def product_kernel(jobs, every, out, right_a, right_b):
+def product_kernel(jobs, every, out, right_a, right_b, peak):
     n_blk = every.shape[0]
     depth = right_a.shape[2]
     unit = depth // n_blk
@@ -57,27 +57,33 @@
 
         @pl.when(is_left)
         def _():
-            for at, wide, dst in panels:
+            for k, (at, wide, dst) in enumerate(panels):
+                most = jnp.zeros((depth, LANES), jnp.float32)
                 for n in range(wide // 2):
                     from_row = pl.multiple_of(depth + unit * at, 2 * unit) + 2 * unit * n
                     pair = every[:, pl.ds(from_row, 2 * unit), :].astype(jnp.float32)
                     for m in range(2):
                         piece = pair[:, unit * m : unit * (m + 1), :].reshape(depth, LANES)
+                        most = jnp.maximum(most, jnp.abs(piece))
                         dst[slot, 2 * n + m] = piece.astype(jnp.bfloat16)
+                peak[slot, k] = jnp.max(most.reshape(depth // 8, 8, LANES), axis=0)
 
         @pl.when(jnp.logical_not(is_left))
         def _():
-            for at, wide, dst in panels:
+            for k, (at, wide, dst) in enumerate(panels):
+                most = jnp.zeros((depth, LANES), jnp.bfloat16)
                 for n in range(wide):
-                    dst[slot, n] = every[at + n, :depth, :]
+                    piece = every[at + n, :depth, :]
+                    most = jnp.maximum(most, jnp.abs(piece))
+                    dst[slot, n] = piece
+                peak[slot, k] = jnp.max(most.astype(jnp.float32).reshape(depth // 8, 8, LANES), axis=0)
 
-    def top(ref, slot):
-        most = jnp.max(jnp.abs(ref[slot]), axis=0).astype(jnp.float32)
-        return jnp.max(most, axis=(0, 1), keepdims=True)
+    def top(slot, k):
+        return jnp.max(peak[slot, k], axis=(0, 1), keepdims=True)
 
     tilt = lax.broadcasted_iota(jnp.int32, (MARK // 2, LANES), 1).astype(jnp.float32) / LANES
     for slot in range(2):
-        bound = jnp.maximum(top(right_a, slot), 2.0**-30) * jnp.maximum(top(right_b, slot), 2.0**-30)
+        bound = jnp.maximum(top(slot, 0), 2.0**-30) * jnp.maximum(top(slot, 1), 2.0**-30)
         power = jnp.ceil(jnp.log2(bound * (depth / 2.0**14))) + fraction
         scale = jnp.where(jobs[slot] < 4 * UT, jnp.exp2(tilt[:1] - power), 0.0)
         places = [chunk(slot * (n_row // 2) + q) for q in range(n_row // 2)]
@@ -107,6 +113,7 @@
         scratch_shapes=[
             pltpu.VMEM((2, wide_a, depth, LANES), jnp.bfloat16),
             pltpu.VMEM((2, wide_b, depth, LANES), jnp.bfloat16),
+            pltpu.VMEM((2, 2, 8, LANES), jnp.float32),
         ],
         compiler_params=pltpu.CompilerParams(vmem_limit_bytes=24 * 2**20),
         cost_estimate=pl.CostEstimate(
@@ -143,7 +150,7 @@
     got = exchange(terms.reshape(side, side, body + MARK, LANES), first)
     power = got[:, :, body:].astype(jnp.float32)
     top = jnp.max(power, axis=0) + 2.0
-    factor = jnp.exp2(power - top)[:, :, :1, :1]
+    factor = jnp.exp2(power - top)[:, :, :1]
     summed = jnp.sum(got[:, :, :body].astype(jnp.float32) * factor, axis=0)
     got = exchange(jnp.concatenate([summed, top], axis=1).astype(jnp.float16), second)
     mark = got[:, body:].astype(jnp.float32)

time: 100 us -> 99.8 us (level)
  no operation moved by 1% of the time
where the time goes in v7:
time: 99.8 us; the launch traced here: 99.5 us
  blocking collectives  93.7 us (94%)
  other arithmetic  3.24 us (3%)
  Pallas kernels  1.96 us (2%)
    all_gather x1, blocking collectives, gathered(): every = lax.all_gather(both, 'blk', axis=0, tiled=False)  51.9 us
    all_to_all x2, blocking collectives, exchange(): lax.all_to_all(terms, ('row', 'blk'), split_axis=0, concat_axis=0, axis_i...  27.9 us
    all_to_all x1, blocking collectives, gathered(): got = lax.all_to_all(out, 'row', split_axis=0, concat_axis=0, tiled=True)  13.9 us

profile of v7, /device:TPU:1, one launch (start us, length us, event | category | flops | bytes accessed | tf_op | source)
XLA Modules:
  0.0 99.5 jit_solution(3402637572123158256)
XLA Ops:
  0.0 0.9 multiply_convert_fusion
  0.9 0.1 copy.7
  1.0 13.9 %all_to_all.15 = f16[16,8,256]{2,1,0:T(8,128)(2,1)S(1)} all-to-all(f16[16,8,256]{2,1,0:T(8,128)(2,1)S(1)} %bitcast.20), channel_id=1, replica_groups=mesh['row'=16,'blk'=32] {'row'}, dimensions={0} | all-to-all | bytes 131072 | tf_op jit(solution)/shard_map/all_to_all | solution.py:25
  14.9 51.9 %all-gather.2 = f16[16384,128]{1,0:T(8,128)(2,1)S(1)} all-gather(f16[512,128]{1,0:T(8,128)(2,1)S(1)} %pad_maximum_fusion.1), channel_id=2, replica_groups=mesh['row'=16,'blk'=32] {'blk'}, dimensions={0}, use_global_device_ids=true | all-gather | bytes 4325376 | tf_op jit(solution)/shard_map/all_gather | solution.py:28
  66.8 0.0 copy-start
  66.8 0.5 convert_element_type.33
  67.3 0.2 copy-done
  67.5 2.0 %shard_map.37 = f32[16,520,128]{2,1,0:T(8,128)S(1)} custom-call(s32[2]{0:T(128)S(1)} %bitcast.16, bf16[32,512,128]{2,1,0:T(8,128)(2,1)S(1)} %bitcast.15), custom_call_target="tpu_custom_call" | custom-call | flops 536870912 | bytes 2097152 | tf_op jit(solution)/shard_map/pallas_call | solution.py:108
  69.5 0.3 convert_element_type.28
  69.7 18.3 %all_to_all.16 = f16[4,4,520,128]{3,2,1,0:T(8,128)(2,1)S(1)} all-to-all(f16[4,4,520,128]{3,2,1,0:T(8,128)(2,1)S(1)} %bitcast.17), channel_id=1, replica_groups={{0,32,64,96},{128,160,192,224},{256,288,320,352},{384,416,448,480},{1,1..., dimensions={0} | all-to-all | bytes 4259840 | tf_op jit(solution)/shard_map/all_to_all | solution.py:144
  88.1 0.0 copy-start.1
  88.1 0.5 multiply_reduce_fusion
  88.6 0.1 convert.6
  88.7 0.1 pad_maximum_fusion
  88.8 9.6 %all_to_all.17 = f16[4,520,128]{2,1,0:T(8,128)(2,1)S(1)} all-to-all(f16[4,520,128]{2,1,0:T(8,128)(2,1)S(1)} %pad_maximum_fusion), channel_id=1, replica_groups={{0,128,256,384},{32,160,288,416},{64,192,320,448},{96,224,352,480},{1,3..., dimensions={0} | all-to-all | bytes 1064960 | tf_op jit(solution)/shard_map/all_to_all | solution.py:144
  98.4 0.1 multiply_reduce_fusion.1
  98.5 0.2 copy.8
  98.7 0.0 copy-done.1
  98.8 0.7 multiply_add_fusion
  (9 shorter events, 0.1 us)
Async XLA Ops:
  66.8 0.7 copy-start
  88.1 10.7 %copy-start.1 = (f32[1,64,1024]{2,1,0:T(8,128)S(1)}, f32[1,64,1024]{2,1,0:T(8,128)}, u32[]{:S(2)}) copy-start(f32[1,64,1024]{2,1,0:T(8,128)} %param.5) | copy-start | bytes 786436

commit v8 on v6

--- a/solution.py
+++ b/solution.py
@@ -1,3 +1,4 @@
+import functools
 import math
 
 import jax
@@ -29,9 +30,9 @@
     return every.astype(jnp.bfloat16)
 
 
-def product_kernel(jobs, every, out, right_a, right_b):
+def product_kernel(jobs, every, out):
     n_blk = every.shape[0]
-    depth = right_a.shape[2]
+    depth = every.shape[1] // 2
     unit = depth // n_blk
     wide_a, wide_b = HALF // LANES, TILE // LANES
     n_row = out.shape[0]
@@ -51,46 +52,49 @@
         j = t - 3 * (t >= 4).astype(jnp.int32) - 2 * (t >= 7).astype(jnp.int32) - (t >= 9).astype(jnp.int32)
         return code < 2 * UT, i * wide_b + lax.rem(within, 2) * wide_a, j * wide_b
 
+    tilt = lax.broadcasted_iota(jnp.int32, (MARK // 2, LANES), 1).astype(jnp.float32) / LANES
+
+    def send(slot, rows, cols):
+        def top(panels):
+            most = functools.reduce(jnp.maximum, [jnp.abs(panel) for panel in panels]).astype(jnp.float32)
+            return jnp.maximum(jnp.max(most, axis=(0, 1), keepdims=True), 2.0**-30)
+
+        power = jnp.ceil(jnp.log2(top(rows) * top(cols) * (depth / 2.0**14))) + fraction
+        scale = jnp.where(jobs[slot] < 4 * UT, jnp.exp2(tilt[:1] - power), 0.0)
+        places = [chunk(slot * (n_row // 2) + q) for q in range(n_row // 2)]
+        for to in places:
+            out[to, wide_b * share :, :] = jnp.concatenate([jnp.broadcast_to(power, tilt.shape), tilt], axis=0)
+        lhs = jnp.concatenate([panel.T for panel in rows], axis=0)
+        for b in range(0, wide_b, 2):
+            rhs = jnp.concatenate([cols[b], cols[b + 1]], axis=1)
+            term = jnp.dot(lhs, rhs, preferred_element_type=jnp.float32)
+            for n in range(2):
+                for q, to in enumerate(places):
+                    piece = term[q * share : (q + 1) * share, n * LANES : (n + 1) * LANES] * scale
+                    out[to, (b + n) * share : (b + n + 1) * share, :] = piece
+
     for slot in range(2):
         is_left, at_a, at_b = place(slot)
-        panels = ((at_a, wide_a, right_a), (at_b, wide_b, right_b))
 
         @pl.when(is_left)
         def _():
-            for at, wide, dst in panels:
+            def load(at, wide):
+                panels = []
                 for n in range(wide // 2):
                     from_row = pl.multiple_of(depth + unit * at, 2 * unit) + 2 * unit * n
                     pair = every[:, pl.ds(from_row, 2 * unit), :].astype(jnp.float32)
                     for m in range(2):
                         piece = pair[:, unit * m : unit * (m + 1), :].reshape(depth, LANES)
-                        dst[slot, 2 * n + m] = piece.astype(jnp.bfloat16)
+                        panels.append(piece.astype(jnp.bfloat16))
+                return panels
+
+            send(slot, load(at_a, wide_a), load(at_b, wide_b))
 
         @pl.when(jnp.logical_not(is_left))
         def _():
-            for at, wide, dst in panels:
-                for n in range(wide):
-                    dst[slot, n] = every[at + n, :depth, :]
-
-    def top(ref, slot):
-        most = jnp.max(jnp.abs(ref[slot]), axis=0).astype(jnp.float32)
-        return jnp.max(most, axis=(0, 1), keepdims=True)
-
-    tilt = lax.broadcasted_iota(jnp.int32, (MARK // 2, LANES), 1).astype(jnp.float32) / LANES
-    for slot in range(2):
-        bound = jnp.maximum(top(right_a, slot), 2.0**-30) * jnp.maximum(top(right_b, slot), 2.0**-30)
-        power = jnp.ceil(jnp.log2(bound * (depth / 2.0**14))) + fraction
-        scale = jnp.where(jobs[slot] < 4 * UT, jnp.exp2(tilt[:1] - power), 0.0)
-        places = [chunk(slot * (n_row // 2) + q) for q in range(n_row // 2)]
-        for to in places:
-            out[to, wide_b * share :, :] = jnp.concatenate([jnp.broadcast_to(power, tilt.shape), tilt], axis=0)
-        lhs = jnp.concatenate([right_a[slot, a].T for a in range(wide_a)], axis=0)
-        for b in range(0, wide_b, 2):
-            rhs = jnp.concatenate([right_b[slot, b], right_b[slot, b + 1]], axis=1)
-            term = jnp.dot(lhs, rhs, preferred_element_type=jnp.float32)
-            for n in range(2):
-                for q, to in enumerate(places):
-                    piece = term[q * share : (q + 1) * share, n * LANES : (n + 1) * LANES] * scale
-                    out[to, (b + n) * share : (b + n + 1) * share, :] = piece
+            rows = [every[at_a + n, :depth, :] for n in range(wide_a)]
+            cols = [every[at_b + n, :depth, :] for n in range(wide_b)]
+            send(slot, rows, cols)
 
 
 def products(jobs, every, n_row):
@@ -104,10 +108,6 @@
         out_shape=jax.ShapeDtypeStruct((n_row, wide_b * share + MARK, LANES), jnp.float32),
         in_specs=[pl.BlockSpec(memory_space=pltpu.SMEM), pl.BlockSpec(memory_space=pltpu.VMEM)],
         out_specs=pl.BlockSpec(memory_space=pltpu.VMEM),
-        scratch_shapes=[
-            pltpu.VMEM((2, wide_a, depth, LANES), jnp.bfloat16),
-            pltpu.VMEM((2, wide_b, depth, LANES), jnp.bfloat16),
-        ],
         compiler_params=pltpu.CompilerParams(vmem_limit_bytes=24 * 2**20),
         cost_estimate=pl.CostEstimate(
             flops=4 * HALF * TILE * depth, bytes_accessed=every.size, transcendentals=0
@@ -143,7 +143,7 @@
     got = exchange(terms.reshape(side, side, body + MARK, LANES), first)
     power = got[:, :, body:].astype(jnp.float32)
     top = jnp.max(power, axis=0) + 2.0
-    factor = jnp.exp2(power - top)[:, :, :1, :1]
+    factor = jnp.exp2(power - top)[:, :, :1]
     summed = jnp.sum(got[:, :, :body].astype(jnp.float32) * factor, axis=0)
     got = exchange(jnp.concatenate([summed, top], axis=1).astype(jnp.float16), second)
     mark = got[:, body:].astype(jnp.float32)

time: 100 us -> 99.3 us (level)
  no operation moved by 1% of the time
where the time goes in v8:
time: 99.3 us; the launch traced here: 99 us
  blocking collectives  93.5 us (94%)
  other arithmetic  3.24 us (3%)
  Pallas kernels  1.71 us (2%)
    all_gather x1, blocking collectives, gathered(): every = lax.all_gather(both, 'blk', axis=0, tiled=False)  51.9 us
    all_to_all x2, blocking collectives, exchange(): lax.all_to_all(terms, ('row', 'blk'), split_axis=0, concat_axis=0, axis_i...  27.7 us
    all_to_all x1, blocking collectives, gathered(): got = lax.all_to_all(out, 'row', split_axis=0, concat_axis=0, tiled=True)  13.9 us

profile of v8, /device:TPU:1, one launch (start us, length us, event | category | flops | bytes accessed | tf_op | source)
XLA Modules:
  0.0 99.0 jit_solution(10965639338612909598)
XLA Ops:
  0.0 0.9 multiply_convert_fusion
  0.9 0.1 copy.7
  1.0 13.9 %all_to_all.15 = f16[16,8,256]{2,1,0:T(8,128)(2,1)S(1)} all-to-all(f16[16,8,256]{2,1,0:T(8,128)(2,1)S(1)} %bitcast.20), channel_id=1, replica_groups=mesh['row'=16,'blk'=32] {'row'}, dimensions={0} | all-to-all | bytes 131072 | tf_op jit(solution)/shard_map/all_to_all | solution.py:26
  14.9 51.9 %all-gather.2 = f16[16384,128]{1,0:T(8,128)(2,1)S(1)} all-gather(f16[512,128]{1,0:T(8,128)(2,1)S(1)} %pad_maximum_fusion.1), channel_id=2, replica_groups=mesh['row'=16,'blk'=32] {'blk'}, dimensions={0}, use_global_device_ids=true | all-gather | bytes 4325376 | tf_op jit(solution)/shard_map/all_gather | solution.py:29
  66.8 0.0 copy-start
  66.8 0.5 convert_element_type.33
  67.3 0.2 copy-done
  67.5 1.7 %shard_map.37 = f32[16,520,128]{2,1,0:T(8,128)S(1)} custom-call(s32[2]{0:T(128)S(1)} %bitcast.16, bf16[32,512,128]{2,1,0:T(8,128)(2,1)S(1)} %bitcast.15), custom_call_target="tpu_custom_call" | custom-call | flops 536870912 | bytes 2097152 | tf_op jit(solution)/shard_map/pallas_call | solution.py:106
  69.2 0.3 convert_element_type.28
  69.5 18.0 %all_to_all.16 = f16[4,4,520,128]{3,2,1,0:T(8,128)(2,1)S(1)} all-to-all(f16[4,4,520,128]{3,2,1,0:T(8,128)(2,1)S(1)} %bitcast.17), channel_id=1, replica_groups={{0,32,64,96},{128,160,192,224},{256,288,320,352},{384,416,448,480},{1,1..., dimensions={0} | all-to-all | bytes 4259840 | tf_op jit(solution)/shard_map/all_to_all | solution.py:137
  87.6 0.0 copy-start.1
  87.6 0.5 multiply_reduce_fusion
  88.0 0.1 convert.6
  88.1 0.1 pad_maximum_fusion
  88.3 9.7 %all_to_all.17 = f16[4,520,128]{2,1,0:T(8,128)(2,1)S(1)} all-to-all(f16[4,520,128]{2,1,0:T(8,128)(2,1)S(1)} %pad_maximum_fusion), channel_id=1, replica_groups={{0,128,256,384},{32,160,288,416},{64,192,320,448},{96,224,352,480},{1,3..., dimensions={0} | all-to-all | bytes 1064960 | tf_op jit(solution)/shard_map/all_to_all | solution.py:137
  98.0 0.1 multiply_reduce_fusion.1
  98.1 0.2 copy.8
  98.3 0.0 copy-done.1
  98.3 0.7 multiply_add_fusion
  (9 shorter events, 0.1 us)
Async XLA Ops:
  66.8 0.7 copy-start
  87.6 10.7 %copy-start.1 = (f32[1,64,1024]{2,1,0:T(8,128)S(1)}, f32[1,64,1024]{2,1,0:T(8,128)}, u32[]{:S(2)}) copy-start(f32[1,64,1024]{2,1,0:T(8,128)} %param.5) | copy-start | bytes 786436

commit v9 on v8

--- a/solution.py
+++ b/solution.py
@@ -13,6 +13,7 @@
 HALF = 512
 UT = 10
 LANES = 128
+SUBLANES = 8
 GAIN = 2.0**15
 MARK = 8
 
@@ -71,7 +72,9 @@
             for n in range(2):
                 for q, to in enumerate(places):
                     piece = term[q * share : (q + 1) * share, n * LANES : (n + 1) * LANES] * scale
-                    out[to, (b + n) * share : (b + n + 1) * share, :] = piece
+                    for i in range(share // SUBLANES):
+                        at = (i * wide_b + b + n) * SUBLANES
+                        out[to, at : at + SUBLANES, :] = piece[i * SUBLANES : (i + 1) * SUBLANES]
 
     for slot in range(2):
         is_left, at_a, at_b = place(slot)
@@ -144,12 +147,12 @@
     power = got[:, :, body:].astype(jnp.float32)
     top = jnp.max(power, axis=0) + 2.0
     factor = jnp.exp2(power - top)[:, :, :1]
-    summed = jnp.sum(got[:, :, :body].astype(jnp.float32) * factor, axis=0)
-    got = exchange(jnp.concatenate([summed, top], axis=1).astype(jnp.float16), second)
+    summed = jnp.sum(got.astype(jnp.float32) * factor, axis=0).astype(jnp.float16)
+    got = exchange(summed.at[:, body:].set(top.astype(jnp.float16)), second)
     mark = got[:, body:].astype(jnp.float32)
     unit = jnp.exp2(mark[:, :1] - mark[:, -1:]) * (4.0 * 0.05 * GAIN**-2)
     summed = jnp.sum(got[:, :body].astype(jnp.float32) * unit, axis=0)
-    summed = summed.reshape(groups, share, LANES).transpose(1, 0, 2).reshape(share, TILE)
+    summed = summed.reshape(share // SUBLANES, groups, SUBLANES, LANES).transpose(0, 2, 1, 3).reshape(share, TILE)
     return 0.95 * old_stats + summed[None]
 
 

time: 99.3 us -> 99 us (level)
  no operation moved by 1% of the time
where the time goes in v9:
time: 99 us; the launch traced here: 98.7 us
  blocking collectives  93.5 us (94%)
  other arithmetic  3.11 us (3%)
  Pallas kernels  1.71 us (2%)
    all_gather x1, blocking collectives, gathered(): every = lax.all_gather(both, 'blk', axis=0, tiled=False)  51.9 us
    all_to_all x2, blocking collectives, exchange(): lax.all_to_all(terms, ('row', 'blk'), split_axis=0, concat_axis=0, axis_i...  27.7 us
    all_to_all x1, blocking collectives, gathered(): got = lax.all_to_all(out, 'row', split_axis=0, concat_axis=0, tiled=True)  13.9 us

profile of v9, /device:TPU:1, one launch (start us, length us, event | category | flops | bytes accessed | tf_op | source)
XLA Modules:
  0.0 98.7 jit_solution(3592503643356949470)
XLA Ops:
  0.0 0.9 multiply_convert_fusion
  0.9 0.1 copy.4
  1.0 13.9 %all_to_all.15 = f16[16,8,256]{2,1,0:T(8,128)(2,1)S(1)} all-to-all(f16[16,8,256]{2,1,0:T(8,128)(2,1)S(1)} %bitcast.22), channel_id=1, replica_groups=mesh['row'=16,'blk'=32] {'row'}, dimensions={0} | all-to-all | bytes 131072 | tf_op jit(solution)/shard_map/all_to_all | solution.py:27
  14.9 51.9 %all-gather.2 = f16[16384,128]{1,0:T(8,128)(2,1)S(1)} all-gather(f16[512,128]{1,0:T(8,128)(2,1)S(1)} %pad_maximum_fusion), channel_id=2, replica_groups=mesh['row'=16,'blk'=32] {'blk'}, dimensions={0}, use_global_device_ids=true | all-gather | bytes 4325376 | tf_op jit(solution)/shard_map/all_gather | solution.py:30
  66.8 0.0 copy-start
  66.8 0.5 convert_element_type.40
  67.3 0.2 copy-done
  67.5 1.7 %shard_map.37 = f32[16,520,128]{2,1,0:T(8,128)S(1)} custom-call(s32[2]{0:T(128)S(1)} %bitcast.18, bf16[32,512,128]{2,1,0:T(8,128)(2,1)S(1)} %bitcast.17), custom_call_target="tpu_custom_call" | custom-call | flops 536870912 | bytes 2097152 | tf_op jit(solution)/shard_map/pallas_call | solution.py:109
  69.2 0.3 convert_element_type.33
  69.5 18.0 %all_to_all.16 = f16[4,4,520,128]{3,2,1,0:T(8,128)(2,1)S(1)} all-to-all(f16[4,4,520,128]{3,2,1,0:T(8,128)(2,1)S(1)} %bitcast.19), channel_id=1, replica_groups={{0,32,64,96},{128,160,192,224},{256,288,320,352},{384,416,448,480},{1,1..., dimensions={0} | all-to-all | bytes 4259840 | tf_op jit(solution)/shard_map/all_to_all | solution.py:140
  87.6 0.5 multiply_reduce_fusion
  88.0 0.0 copy-start.1
  88.1 0.1 convert_element_type.36
  88.2 9.7 %all_to_all.17 = f16[4,520,128]{2,1,0:T(8,128)(2,1)S(1)} all-to-all(f16[4,520,128]{2,1,0:T(8,128)(2,1)S(1)} %convert_dynamic-update-slice_fusion), channel_id=1, replica_groups={{0,128,256,384},{32,160,288,416},{64,192,320,448},{96,224,352,480},{1,3..., dimensions={0} | all-to-all | bytes 1064960 | tf_op jit(solution)/shard_map/all_to_all | solution.py:140
  97.9 0.1 multiply_reduce_fusion.1
  98.0 0.0 copy-done.1
  98.0 0.7 multiply_add_fusion
  (9 shorter events, 0.1 us)
Async XLA Ops:
  66.8 0.7 copy-start
  88.0 9.9 %copy-start.1 = (f32[1,64,1024]{2,1,0:T(8,128)S(1)}, f32[1,64,1024]{2,1,0:T(8,128)}, u32[]{:S(2)}) copy-start(f32[1,64,1024]{2,1,0:T(8,128)} %param.7) | copy-start | bytes 786436

commit v10 on v9

--- a/solution.py
+++ b/solution.py
@@ -60,7 +60,7 @@
             most = functools.reduce(jnp.maximum, [jnp.abs(panel) for panel in panels]).astype(jnp.float32)
             return jnp.maximum(jnp.max(most, axis=(0, 1), keepdims=True), 2.0**-30)
 
-        power = jnp.ceil(jnp.log2(top(rows) * top(cols) * (depth / 2.0**14))) + fraction
+        power = jnp.ceil(jnp.log2(top(rows) * top(cols) * (depth / 2.0**12))) + fraction
         scale = jnp.where(jobs[slot] < 4 * UT, jnp.exp2(tilt[:1] - power), 0.0)
         places = [chunk(slot * (n_row // 2) + q) for q in range(n_row // 2)]
         for to in places:
@@ -144,13 +144,13 @@
     every = gathered(gradient)
     terms = products(slot_jobs[0], every, n_row).astype(jnp.float16)
     got = exchange(terms.reshape(side, side, body + MARK, LANES), first)
-    power = got[:, :, body:].astype(jnp.float32)
-    top = jnp.max(power, axis=0) + 2.0
-    factor = jnp.exp2(power - top)[:, :, :1]
+    mark = got[:, :, body:]
+    top = jnp.max(mark, axis=0)
+    factor = jnp.exp2(mark[:, :, :1].astype(jnp.float32) - top[:, :1].astype(jnp.float32))
     summed = jnp.sum(got.astype(jnp.float32) * factor, axis=0).astype(jnp.float16)
-    got = exchange(summed.at[:, body:].set(top.astype(jnp.float16)), second)
+    got = exchange(summed.at[:, body:].set(top), second)
     mark = got[:, body:].astype(jnp.float32)
-    unit = jnp.exp2(mark[:, :1] - mark[:, -1:]) * (4.0 * 0.05 * GAIN**-2)
+    unit = jnp.exp2(mark[:, :1] - mark[:, -1:]) * (0.05 * GAIN**-2)
     summed = jnp.sum(got[:, :body].astype(jnp.float32) * unit, axis=0)
     summed = summed.reshape(share // SUBLANES, groups, SUBLANES, LANES).transpose(0, 2, 1, 3).reshape(share, TILE)
     return 0.95 * old_stats + summed[None]

time: 99 us -> 98.9 us (level)
  no operation moved by 1% of the time
where the time goes in v10:
time: 98.9 us; the launch traced here: 98.7 us
  blocking collectives  93.5 us (95%)
  other arithmetic  3.1 us (3%)
  Pallas kernels  1.69 us (2%)
    all_gather x1, blocking collectives, gathered(): every = lax.all_gather(both, 'blk', axis=0, tiled=False)  51.9 us
    all_to_all x2, blocking collectives, exchange(): lax.all_to_all(terms, ('row', 'blk'), split_axis=0, concat_axis=0, axis_i...  27.7 us
    all_to_all x1, blocking collectives, gathered(): got = lax.all_to_all(out, 'row', split_axis=0, concat_axis=0, tiled=True)  13.9 us

profile of v10, /device:TPU:1, one launch (start us, length us, event | category | flops | bytes accessed | tf_op | source)
XLA Modules:
  0.0 98.7 jit_solution(9040368564472177162)
XLA Ops:
  0.0 0.9 multiply_convert_fusion
  0.9 0.1 copy.5
  1.0 13.9 %all_to_all.15 = f16[16,8,256]{2,1,0:T(8,128)(2,1)S(1)} all-to-all(f16[16,8,256]{2,1,0:T(8,128)(2,1)S(1)} %bitcast.23), channel_id=1, replica_groups=mesh['row'=16,'blk'=32] {'row'}, dimensions={0} | all-to-all | bytes 131072 | tf_op jit(solution)/shard_map/all_to_all | solution.py:27
  14.9 51.9 %all-gather.2 = f16[16384,128]{1,0:T(8,128)(2,1)S(1)} all-gather(f16[512,128]{1,0:T(8,128)(2,1)S(1)} %pad_maximum_fusion), channel_id=2, replica_groups=mesh['row'=16,'blk'=32] {'blk'}, dimensions={0}, use_global_device_ids=true | all-gather | bytes 4325376 | tf_op jit(solution)/shard_map/all_gather | solution.py:30
  66.8 0.0 copy-start
  66.8 0.5 convert_element_type.37
  67.3 0.2 copy-done
  67.5 1.7 %shard_map.37 = f32[16,520,128]{2,1,0:T(8,128)S(1)} custom-call(s32[2]{0:T(128)S(1)} %bitcast.19, bf16[32,512,128]{2,1,0:T(8,128)(2,1)S(1)} %bitcast.18), custom_call_target="tpu_custom_call" | custom-call | flops 536870912 | bytes 2097152 | tf_op jit(solution)/shard_map/pallas_call | solution.py:109
  69.2 0.3 convert_element_type.31
  69.5 18.0 %all_to_all.16 = f16[4,4,520,128]{3,2,1,0:T(8,128)(2,1)S(1)} all-to-all(f16[4,4,520,128]{3,2,1,0:T(8,128)(2,1)S(1)} %bitcast.20), channel_id=1, replica_groups={{0,32,64,96},{128,160,192,224},{256,288,320,352},{384,416,448,480},{1,1..., dimensions={0} | all-to-all | bytes 4259840 | tf_op jit(solution)/shard_map/all_to_all | solution.py:140
  87.5 0.5 multiply_reduce_fusion
  88.0 0.0 copy-start.1
  88.0 0.1 convert_element_type.34
  88.1 9.7 %all_to_all.17 = f16[4,520,128]{2,1,0:T(8,128)(2,1)S(1)} all-to-all(f16[4,520,128]{2,1,0:T(8,128)(2,1)S(1)} %constant_dynamic-update-slice_fusion), channel_id=1, replica_groups={{0,128,256,384},{32,160,288,416},{64,192,320,448},{96,224,352,480},{1,3..., dimensions={0} | all-to-all | bytes 1064960 | tf_op jit(solution)/shard_map/all_to_all | solution.py:140
  97.8 0.1 multiply_reduce_fusion.1
  97.9 0.0 copy-done.1
  97.9 0.7 multiply_add_fusion
  (7 shorter events, 0.1 us)
Async XLA Ops:
  66.8 0.7 copy-start
  88.0 9.9 %copy-start.1 = (f32[1,64,1024]{2,1,0:T(8,128)S(1)}, f32[1,64,1024]{2,1,0:T(8,128)}, u32[]{:S(2)}) copy-start(f32[1,64,1024]{2,1,0:T(8,128)} %param.7) | copy-start | bytes 786436

commit v11 on v10

--- a/solution.py
+++ b/solution.py
@@ -147,7 +147,7 @@
     mark = got[:, :, body:]
     top = jnp.max(mark, axis=0)
     factor = jnp.exp2(mark[:, :, :1].astype(jnp.float32) - top[:, :1].astype(jnp.float32))
-    summed = jnp.sum(got.astype(jnp.float32) * factor, axis=0).astype(jnp.float16)
+    summed = sum(got[n].astype(jnp.float32) * factor[n] for n in range(side)).astype(jnp.float16)
     got = exchange(summed.at[:, body:].set(top), second)
     mark = got[:, body:].astype(jnp.float32)
     unit = jnp.exp2(mark[:, :1] - mark[:, -1:]) * (0.05 * GAIN**-2)

time: 98.9 us -> 99 us (level)
  no operation moved by 1% of the time
where the time goes in v11:
time: 99 us; the launch traced here: 98.7 us
  blocking collectives  93.6 us (95%)
  other arithmetic  3.01 us (3%)
  Pallas kernels  1.71 us (2%)
    all_gather x1, blocking collectives, gathered(): every = lax.all_gather(both, 'blk', axis=0, tiled=False)  51.9 us
    all_to_all x2, blocking collectives, exchange(): lax.all_to_all(terms, ('row', 'blk'), split_axis=0, concat_axis=0, axis_i...  27.8 us
    all_to_all x1, blocking collectives, gathered(): got = lax.all_to_all(out, 'row', split_axis=0, concat_axis=0, tiled=True)  13.9 us

profile of v11, /device:TPU:1, one launch (start us, length us, event | category | flops | bytes accessed | tf_op | source)
XLA Modules:
  0.0 98.7 jit_solution(4426831944328926062)
XLA Ops:
  0.0 0.9 multiply_convert_fusion
  0.9 0.1 copy.4
  1.0 13.9 %all_to_all.15 = f16[16,8,256]{2,1,0:T(8,128)(2,1)S(1)} all-to-all(f16[16,8,256]{2,1,0:T(8,128)(2,1)S(1)} %bitcast.46), channel_id=1, replica_groups=mesh['row'=16,'blk'=32] {'row'}, dimensions={0} | all-to-all | bytes 131072 | tf_op jit(solution)/shard_map/all_to_all | solution.py:27
  14.9 51.9 %all-gather.2 = f16[16384,128]{1,0:T(8,128)(2,1)S(1)} all-gather(f16[512,128]{1,0:T(8,128)(2,1)S(1)} %pad_maximum_fusion), channel_id=2, replica_groups=mesh['row'=16,'blk'=32] {'blk'}, dimensions={0}, use_global_device_ids=true | all-gather | bytes 4325376 | tf_op jit(solution)/shard_map/all_gather | solution.py:30
  66.8 0.0 copy-start
  66.8 0.5 convert_element_type.69
  67.3 0.2 copy-done
  67.5 1.7 %shard_map.37 = f32[16,520,128]{2,1,0:T(8,128)S(1)} custom-call(s32[2]{0:T(128)S(1)} %bitcast.42, bf16[32,512,128]{2,1,0:T(8,128)(2,1)S(1)} %bitcast.41), custom_call_target="tpu_custom_call" | custom-call | flops 536870912 | bytes 2097152 | tf_op jit(solution)/shard_map/pallas_call | solution.py:109
  69.2 0.3 convert_element_type.52
  69.5 18.0 %all_to_all.16 = f16[4,4,520,128]{3,2,1,0:T(8,128)(2,1)S(1)} all-to-all(f16[4,4,520,128]{3,2,1,0:T(8,128)(2,1)S(1)} %bitcast.43), channel_id=1, replica_groups={{0,32,64,96},{128,160,192,224},{256,288,320,352},{384,416,448,480},{1,1..., dimensions={0} | all-to-all | bytes 4259840 | tf_op jit(solution)/shard_map/all_to_all | solution.py:140
  87.6 0.5 fusion.1
  88.0 0.0 copy-start.1
  88.0 9.8 %all_to_all.17 = f16[4,520,128]{2,1,0:T(8,128)(2,1)S(1)} all-to-all(f16[4,520,128]{2,1,0:T(8,128)(2,1)S(1)} %constant_dynamic-update-slice_fusion), channel_id=1, replica_groups={{0,128,256,384},{32,160,288,416},{64,192,320,448},{96,224,352,480},{1,3..., dimensions={0} | all-to-all | bytes 1064960 | tf_op jit(solution)/shard_map/all_to_all | solution.py:140
  97.9 0.1 multiply_reduce_fusion
  98.0 0.0 copy-done.1
  98.0 0.7 multiply_add_fusion
  (8 shorter events, 0.1 us)
Async XLA Ops:
  66.8 0.7 copy-start
  88.0 10.0 %copy-start.1 = (f32[1,64,1024]{2,1,0:T(8,128)S(1)}, f32[1,64,1024]{2,1,0:T(8,128)}, u32[]{:S(2)}) copy-start(f32[1,64,1024]{2,1,0:T(8,128)} %param.7) | copy-start | bytes 786436
